TPU v7x, 32 devices: a whole 2x2x4 slice. The times are simulated.
32 devices in a mesh: dp: 4 (over z), row: 2 (over x), col: 4 (over y, core).
Axes of the slice: x: 2, y: 2, z: 4, core: 2. Of those that a mesh axis runs over, the one named last changes fastest.
Arguments:
- inputs: bfloat16 [4, 192, 16, 512], P('dp', None, 'row', 'col'), may hold values from -16 to 16
- norm_gain: float32 [192], replicated, may hold values from 0.25 to 1.75
- w_expand: bfloat16 [192, 768], replicated, may hold values from -0.4375 to 0.4375
- kernel: float32 [768, 9], replicated, may hold values from -2 to 2
- w_squeeze: float32 [768, 48], replicated, may hold values from -1.5 to 1.5
- w_excite: float32 [48, 768], replicated, may hold values from -6 to 6
- w_project: bfloat16 [768, 192], replicated, may hold values from -0.21875 to 0.21875
- cotangent: bfloat16 [4, 192, 16, 512], P('dp', None, 'row', 'col'), may hold values from -16 to 16
Outputs:
- output: bfloat16 [4, 192, 16, 512], P('dp', None, 'row', 'col')
- grad_inputs: bfloat16 [4, 192, 16, 512], P('dp', None, 'row', 'col')
- grad_gain: float32 [192], replicated
- grad_w_expand: float32 [192, 768], replicated
- grad_kernel: float32 [768, 9], replicated
- grad_w_squeeze: float32 [768, 48], replicated
- grad_w_excite: float32 [48, 768], replicated
- grad_w_project: float32 [768, 192], replicated
All inputs are finite; a program needn't handle non-finite values.
Results may differ from a plain program's by a relative error of at most 0.0019.
Values may be sent and summed in bfloat16 or wider, within the bound.
A program may use at most 64 MiB of HBM per device.

v0:
```python
import jax
import jax.numpy as jnp
from jax import lax
from jax.sharding import PartitionSpec as P

EPS = 1e-06
HIGH = lax.Precision.HIGHEST


def with_halo(shard, sides, width):
    for axis, dim in sides:
        count, length = (lax.axis_size(axis), shard.shape[dim])
        up = [(i, (i + 1) % count) for i in range(count - 1)]
        down = [(j, i) for i, j in up]
        last = lax.slice_in_dim(shard, length - width, length, axis=dim)
        leading = lax.slice_in_dim(shard, 0, width, axis=dim)
        before = lax.ppermute(last, axis, up)
        after = lax.ppermute(leading, axis, down)
        shard = jnp.concatenate([before, shard, after], axis=dim)
    return shard


def silu_slope(value):
    sig = jax.nn.sigmoid(value)
    return sig * (1.0 + value * (1.0 - sig))


def normalize(inputs, norm_gain):
    widened = inputs.astype(jnp.float32)
    inverse = lax.rsqrt(jnp.mean(widened * widened, axis=1, keepdims=True) + EPS)
    normed = widened * inverse
    scaled = (normed * norm_gain[None, :, None, None]).astype(jnp.bfloat16)
    return (normed, inverse, scaled)


def expand(scaled, w_expand):
    return jnp.einsum("bchw,ce->behw", scaled, w_expand, preferred_element_type=jnp.float32)


def depthwise(hidden_pad, kernel, out_rows, out_cols):
    total = jnp.zeros((hidden_pad.shape[0], hidden_pad.shape[1], out_rows, out_cols), jnp.float32)
    for tap in range(9):
        drow, dcol = (tap // 3, tap % 3)
        total = (
            total
            + kernel[:, tap][None, :, None, None]
            * hidden_pad[:, :, drow : drow + out_rows, dcol : dcol + out_cols]
        )
    return total


def local(inputs, norm_gain, w_expand, kernel, w_squeeze, w_excite, w_project, cotangent):
    batch, chans, rows, cols = inputs.shape
    pixels = rows * cols * lax.axis_size("row") * lax.axis_size("col")
    normed, inverse, scaled = normalize(inputs, norm_gain)
    pre = expand(scaled, w_expand)
    hidden = jax.nn.silu(pre).astype(jnp.bfloat16)
    hidden_pad = with_halo(hidden, (("row", 2), ("col", 3)), 1)
    conv = depthwise(hidden_pad, kernel, rows, cols)
    act = jax.nn.silu(conv)
    pooled = lax.psum(jnp.sum(act, axis=(2, 3)), ("row", "col")) / pixels
    squeeze_pre = jnp.dot(pooled, w_squeeze, precision=HIGH)
    squeezed = jax.nn.silu(squeeze_pre)
    excite_pre = jnp.dot(squeezed, w_excite, precision=HIGH)
    excite = jax.nn.sigmoid(excite_pre)
    gated = (act * excite[:, :, None, None]).astype(jnp.bfloat16)
    proj = jnp.einsum("behw,ec->bchw", gated, w_project, preferred_element_type=jnp.float32)
    output = (inputs.astype(jnp.float32) + proj).astype(jnp.bfloat16)
    grad_gated = jnp.einsum(
        "bchw,ec->behw", cotangent, w_project, preferred_element_type=jnp.float32
    )
    grad_project = jnp.einsum("behw,bchw->ec", gated, cotangent, preferred_element_type=jnp.float32)
    grad_excite = lax.psum(jnp.sum(grad_gated * act, axis=(2, 3)), ("row", "col"))
    grad_epre = grad_excite * excite * (1.0 - excite)
    grad_wexc = jnp.einsum("bs,be->se", squeezed, grad_epre, precision=HIGH)
    grad_spre = jnp.einsum("be,se->bs", grad_epre, w_excite, precision=HIGH) * silu_slope(
        squeeze_pre
    )
    grad_wsq = jnp.einsum("be,bs->es", pooled, grad_spre, precision=HIGH)
    grad_pooled = jnp.einsum("bs,es->be", grad_spre, w_squeeze, precision=HIGH)
    grad_act = grad_gated * excite[:, :, None, None] + (grad_pooled / pixels)[:, :, None, None]
    grad_conv = (grad_act * silu_slope(conv)).astype(jnp.bfloat16)
    grad_pad = with_halo(grad_conv, (("row", 2), ("col", 3)), 1)
    grad_hidden = jnp.zeros(pre.shape, jnp.float32)
    taps = []
    for tap in range(9):
        drow, dcol = (tap // 3, tap % 3)
        grad_hidden = (
            grad_hidden
            + kernel[:, tap][None, :, None, None]
            * grad_pad[:, :, 2 - drow : 2 - drow + rows, 2 - dcol : 2 - dcol + cols]
        )
        taps.append(
            jnp.sum(
                grad_conv.astype(jnp.float32)
                * hidden_pad[:, :, drow : drow + rows, dcol : dcol + cols].astype(jnp.float32),
                axis=(0, 2, 3),
            )
        )
    grad_kernel = jnp.stack(taps, axis=1)
    grad_pre = (grad_hidden * silu_slope(pre)).astype(jnp.bfloat16)
    grad_wexp = jnp.einsum("bchw,behw->ce", scaled, grad_pre, preferred_element_type=jnp.float32)
    grad_scaled = jnp.einsum(
        "ce,behw->bchw", w_expand, grad_pre, preferred_element_type=jnp.float32
    )
    grad_gain = jnp.sum(grad_scaled * normed, axis=(0, 2, 3))
    grad_normed = grad_scaled * norm_gain[None, :, None, None]
    grad_in = inverse * (
        grad_normed - normed * jnp.mean(grad_normed * normed, axis=1, keepdims=True)
    ) + cotangent.astype(jnp.float32)
    grad_wsq_all, grad_wexc_all = lax.psum((grad_wsq, grad_wexc), "dp")
    gain_all, wexp_all, kernel_all, project_all = lax.psum(
        (grad_gain, grad_wexp, grad_kernel, grad_project), ("dp", "row", "col")
    )
    return (
        output,
        grad_in.astype(jnp.bfloat16),
        gain_all,
        wexp_all,
        kernel_all,
        grad_wsq_all,
        grad_wexc_all,
        project_all,
    )


def solution(mesh):
    placed = (
        P("dp", None, "row", "col"),
        P(),
        P(),
        P(),
        P(),
        P(),
        P(),
        P("dp", None, "row", "col"),
    )
    return jax.shard_map(
        local,
        mesh=mesh,
        in_specs=placed,
        out_specs=(
            P("dp", None, "row", "col"),
            P("dp", None, "row", "col"),
            P(),
            P(),
            P(),
            P(),
            P(),
            P(),
        ),
        check_vma=False,
    )
```

profile of v0, /device:TPU:0, one launch (start us, length us, event | category | flops | bytes accessed | tf_op | source)
XLA Modules:
  0.0 271.2 jit_solution(5628280988328780552)
XLA Ops:
  7.2 1.1 fusion.59
  8.4 3.8 %fusion.30 = (bf16[768,8,128]{0,2,1:T(8,128)(2,1)S(1)}, f32[8,128,768]{2,1,0:T(8,128)}) fusion(bf16[192,768]{1,0:T(8,128)(2,1)} %param.10, f32[192]{0:T(256)} %param.9, f32[8,128]{1,0:T(8,128)S(1)} %add_rsqrt_fusion, bf16[1,192,8,128]{3,2,1,0:T(8,128)(2,1)} %param.8), kind=kOutput, calls=%fused_computation.55 | convolution fusion | flops 306708480 | bytes 5411584 | tf_op jit(solution)/shard_map/bchw,ce->behw/dot_general | solution.py:37
  12.2 4.9 %collective-permute-start = (bf16[1,768,1,128]{1,3,2,0:T(8,128)(2,1)S(1)}, bf16[1,768,1,128]{1,3,2,0:T(8,128)(2,1)S(1)}, u32[]{:S(2)}, u32[]{:S(2)}) collective-permute-start(bf16[1,768,1,128]{1,3,2,0:T(8,128)(2,1)S(1)} %get-tuple-element.65), channel_id=1, source_target_pairs={{0,4},{1,5},{2,6},{3,7},{8,12},{9,13},{10,14},{11,15},{16,20},{17,... | collective-permute-start | bytes 589832 | tf_op jit(solution)/shard_map/ppermute | solution.py:17
  17.1 1.3 collective-permute-start.1
  18.4 2.8 %collective-permute-done = bf16[1,768,1,128]{1,3,2,0:T(8,128)(2,1)S(1)} collective-permute-done((bf16[1,768,1,128]{1,3,2,0:T(8,128)(2,1)S(1)}, bf16[1,768,1,128]{1,3,2,0:T(8,128)(2,1)S(1)}, u32[]{:S(2)}, u32[]{:S(2)}) %collective-permute-start) | collective-permute-done | bytes 196640 | tf_op jit(solution)/shard_map/ppermute | solution.py:17
  21.2 4.1 %collective-permute-done.1 = bf16[1,768,1,128]{1,3,2,0:T(8,128)(2,1)S(1)} collective-permute-done((bf16[1,768,1,128]{1,3,2,0:T(8,128)(2,1)S(1)}, bf16[1,768,1,128]{1,3,2,0:T(8,128)(2,1)S(1)}, u32[]{:S(2)}, u32[]{:S(2)}) %collective-permute-start.1) | collective-permute-done | bytes 196640 | tf_op jit(solution)/shard_map/ppermute | solution.py:18
  25.4 1.3 collective-permute-start.2
  26.7 1.4 collective-permute-start.3
  28.2 3.4 %collective-permute-done.3 = bf16[1,768,10,1]{1,3,2,0:T(2,128)(2,1)S(1)} collective-permute-done((bf16[1,768,10,1]{1,3,2,0:T(2,128)(2,1)S(1)}, bf16[1,768,10,1]{1,3,2,0:T(2,128)(2,1)S(1)}, u32[]{:S(2)}, u32[]{:S(2)}) %collective-permute-start.3) | collective-permute-done | bytes 15392 | tf_op jit(solution)/shard_map/ppermute | solution.py:18
  32.7 7.2 %fusion.26 = (f32[768]{0:T(1024)S(1)}, f32[768]{0:T(1024)S(1)}, f32[1,768,8,128]{1,3,2,0:T(8,128)}, f32[768,8,128]{0,2,1:T(8,128)}) fusion(bf16[1,768,10,129]{1,3,2,0:T(8,128)(2,1)S(1)} %get-tuple-element.60, f32[768]{0:T(1024)S(1)} %get-tuple-element.41, bf16[1,768,1,128]{1,3,2,0:T(8,128)(2,1)S(1)} %collective-permute-done.1, ...), kind=kOutput, calls=%fused_computation.48 | convolution fusion | flops 329513472 | bytes 19989504 | tf_op jit(solution)/shard_map/bchw,ec->behw/dot_general | solution.py:69
  39.9 14.6 %all-reduce.2 = (f32[1,768]{1,0:T(1,128)S(1)}, f32[1,768]{1,0:T(1,128)S(1)}) all-reduce(f32[1,768]{1,0:T(1,128)S(1)} %reduce_sum.132, f32[1,768]{1,0:T(1,128)S(1)} %reduce_sum.134), channel_id=1, replica_groups=mesh['dp'=4,'row'=2,'col'=4] {'row','col'}, use_global_device_ids=true, to_apply=%region_2.3 | all-reduce | flops 1536 | bytes 12288 | tf_op jit(solution)/shard_map/psum | solution.py:61
  55.1 3.9 %fusion.46 = bf16[1,192,8,128]{3,1,2,0:T(8,128)(2,1)} fusion(f32[768]{0:T(1024)S(1)} %get-tuple-element.68, bf16[768,192]{0,1:T(8,128)(2,1)S(1)} %copy-done, bf16[1,192,8,128]{3,2,1,0:T(8,128)(2,1)S(1)} %copy-done.13, f32[1,768,8,128]{1,3,2,0:T(8,128)} %get-tuple-element.54), kind=kOutput, calls=%fused_computation.79 | convolution fusion | flops 307298304 | bytes 4230144 | tf_op jit(solution)/shard_map/behw,ec->bchw/dot_general | solution.py:67
  59.0 1.9 convolution_bitcast_fusion.1
  62.3 5.6 %fusion.24 = (f32[768]{0:T(1024)S(1)}, f32[768]{0:T(1024)S(1)}, f32[768]{0:T(1024)S(1)}, f32[768]{0:T(1024)S(1)}, f32[768]{0:T(1024)S(1)}, /*index=5*/f32[768]{0...) fusion(bf16[1,768,10,129]{1,3,2,0:T(8,128)(2,1)S(1)} %copy-done.4, ...), kind=kLoop, calls=%fused_computation.44 | loop fusion | flops 32236800 | bytes 20874240 | tf_op jit(solution)/shard_map/reduce_sum | solution.py:94
  68.0 1.9 collective-permute-start.4
  69.9 1.3 collective-permute-start.5
  72.0 1.1 collective-permute-done.4
  73.1 4.4 %collective-permute-done.5 = bf16[1,768,1,128]{1,3,2,0:T(8,128)(2,1)S(1)} collective-permute-done((bf16[1,768,1,128]{1,3,2,0:T(8,128)(2,1)S(1)}, bf16[1,768,1,128]{1,3,2,0:T(8,128)(2,1)S(1)}, u32[]{:S(2)}, u32[]{:S(2)}) %collective-permute-start.5) | collective-permute-done | bytes 196640 | tf_op jit(solution)/shard_map/ppermute | solution.py:18
  77.6 1.3 collective-permute-start.6
  78.9 3.0 %collective-permute-start.7 = (bf16[1,768,10,1]{1,3,2,0:T(2,128)(2,1)S(1)}, bf16[1,768,10,1]{1,3,2,0:T(2,128)(2,1)S(1)}, u32[]{:S(2)}, u32[]{:S(2)}) collective-permute-start(bf16[1,768,10,1]{1,3,2,0:T(2,128)(2,1)S(1)} %get-tuple-element.58), channel_id=1, source_target_pairs={{0,1},{1,2},{2,3},{4,5},{5,6},{6,7},{8,9},{9,10},{10,11},{12,13},{... | collective-permute-start | bytes 46088 | tf_op jit(solution)/shard_map/ppermute | solution.py:17
  82.7 1.0 copy.24
  86.0 4.7 %fusion.15 = bf16[1,768,8,128]{1,3,2,0:T(8,128)(2,1)S(1)} fusion(bf16[1,768,8,128]{1,3,2,0:T(8,128)(2,1)S(1)} %get-tuple-element.53, f32[8,128,768]{2,1,0:T(8,128)S(1)} %copy-done.5, bf16[1,768,10,129]{1,3,2,0:T(8,128)(2,1)S(1)} %get-tuple-element.56, bf16[1,768,1,128]{1,3,2,0:T(8,128)(2,1)S(1)} %collective-permute-done.4, ...), kind=kLoop, calls=%fused_computation.35 | loop fusion | flops 29097984 | bytes 16149504 | tf_op jit(solution)/shard_map/convert_element_type | solution.py:101
  90.7 1.1 copy-done.12
  91.9 1.4 fusion.43
  93.3 2.2 fusion.58
  95.7 1.0 copy.25
  96.7 41.0 %all-reduce = (f32[192]{0:T(256)}, f32[768,9]{0,1:T(8,128)}) all-reduce(f32[192]{0:T(256)S(1)} %get-tuple-element.32, f32[768,9]{0,1:T(8,128)S(1)} %stack.39), channel_id=1, replica_groups=mesh['dp'=4,'row'=2,'col'=4] {'dp','row','col'}, use_global_device_ids=true, to_apply=%region_7.8 | all-reduce | flops 7104 | bytes 56832 | tf_op jit(solution)/shard_map/psum | solution.py:112
  137.8 119.6 %all-reduce.7.cloned.1.call-done = (f32[192,768]{1,0:T(8,128)}, f32[768,192]{0,1:T(8,128)}) async-done(((f32[192,768]{1,0:T(8,128)}, f32[768,192]{0,1:T(8,128)}), (f32[192,768]{1,0:T(8,128)}, f32[768,192]{0,1:T(8,128)})) %all-reduce.7.cloned.1.call-update) | async-done | bytes 1179664 | tf_op jit(solution)/shard_map/psum | solution.py:112
  257.4 1.9 copy.51
  259.3 1.6 copy.52
  260.9 1.6 copy.53
  262.5 1.9 copy.54
  (84 shorter events, 7.0 us)
Async XLA Ops:
  7.2 25.5 %copy-start = (bf16[768,192]{0,1:T(8,128)(2,1)S(1)}, bf16[768,192]{0,1:T(8,128)(2,1)}, u32[]{:S(2)}) copy-start(bf16[768,192]{0,1:T(8,128)(2,1)} %param.14) | copy-start | bytes 884740
  7.2 130.6 %all-reduce.9.cloned.1.call-start = ((), (), s32[]{:S(2)}) async-start(), calls=%async_computation.1 | async-start | bytes 589824 | tf_op jit(solution)/shard_map/psum | solution.py:111
  8.4 19.8 %copy-start.20 = (f32[768,9]{0,1:T(8,128)S(1)}, f32[768,9]{0,1:T(8,128)}, u32[]{:S(2)}) copy-start(f32[768,9]{0,1:T(8,128)} %param.11) | copy-start | bytes 82948
  12.2 9.0 %collective-permute-start = (bf16[1,768,1,128]{1,3,2,0:T(8,128)(2,1)S(1)}, bf16[1,768,1,128]{1,3,2,0:T(8,128)(2,1)S(1)}, u32[]{:S(2)}, u32[]{:S(2)}) collective-permute-start(bf16[1,768,1,128]{1,3,2,0:T(8,128)(2,1)S(1)} %get-tuple-element.65), channel_id=1, source_target_pairs={{0,4},{1,5},{2,6},{3,7},{8,12},{9,13},{10,14},{11,15},{16,20},{17,... | collective-permute-start | bytes 589832 | tf_op jit(solution)/shard_map/ppermute | solution.py:17
  17.1 8.3 %collective-permute-start.1 = (bf16[1,768,1,128]{1,3,2,0:T(8,128)(2,1)S(1)}, bf16[1,768,1,128]{1,3,2,0:T(8,128)(2,1)S(1)}, u32[]{:S(2)}, u32[]{:S(2)}) collective-permute-start(bf16[1,768,1,128]{1,3,2,0:T(8,128)(2,1)S(1)} %get-tuple-element.66), channel_id=1, source_target_pairs={{4,0},{5,1},{6,2},{7,3},{12,8},{13,9},{14,10},{15,11},{20,16},{21,... | collective-permute-start | bytes 589832 | tf_op jit(solution)/shard_map/ppermute | solution.py:18
  21.2 11.4 %copy-start.8 = (bf16[1,768,1,128]{1,3,2,0:T(8,128)(2,1)}, bf16[1,768,1,128]{1,3,2,0:T(8,128)(2,1)S(1)}, u32[]{:S(2)}) copy-start(bf16[1,768,1,128]{1,3,2,0:T(8,128)(2,1)S(1)} %collective-permute-done) | copy-start | bytes 589828
  25.3 7.3 %copy-start.10 = (bf16[1,768,1,128]{1,3,2,0:T(8,128)(2,1)}, bf16[1,768,1,128]{1,3,2,0:T(8,128)(2,1)S(1)}, u32[]{:S(2)}) copy-start(bf16[1,768,1,128]{1,3,2,0:T(8,128)(2,1)S(1)} %collective-permute-done.1) | copy-start | bytes 589828
  25.4 2.8 %collective-permute-start.2 = (bf16[1,768,10,1]{1,3,2,0:T(2,128)(2,1)S(1)}, bf16[1,768,10,1]{1,3,2,0:T(2,128)(2,1)S(1)}, u32[]{:S(2)}, u32[]{:S(2)}) collective-permute-start(bf16[1,768,10,1]{1,3,2,0:T(2,128)(2,1)S(1)} %get-tuple-element.61), channel_id=1, source_target_pairs={{0,1},{1,2},{2,3},{4,5},{5,6},{6,7},{8,9},{9,10},{10,11},{12,13},{... | collective-permute-start | bytes 46088 | tf_op jit(solution)/shard_map/ppermute | solution.py:17
  26.7 6.0 %copy-start.17 = (bf16[1,192,8,128]{3,2,1,0:T(8,128)(2,1)S(1)}, bf16[1,192,8,128]{3,2,1,0:T(8,128)(2,1)}, u32[]{:S(2)}) copy-start(bf16[1,192,8,128]{3,2,1,0:T(8,128)(2,1)} %param.15) | copy-start | bytes 1179652
  26.7 5.0 %collective-permute-start.3 = (bf16[1,768,10,1]{1,3,2,0:T(2,128)(2,1)S(1)}, bf16[1,768,10,1]{1,3,2,0:T(2,128)(2,1)S(1)}, u32[]{:S(2)}, u32[]{:S(2)}) collective-permute-start(bf16[1,768,10,1]{1,3,2,0:T(2,128)(2,1)S(1)} %get-tuple-element.62), channel_id=1, source_target_pairs={{1,0},{2,1},{3,2},{5,4},{6,5},{7,6},{9,8},{10,9},{11,10},{13,12},{... | collective-permute-start | bytes 46088 | tf_op jit(solution)/shard_map/ppermute | solution.py:18
  32.6 7.3 %copy-start.1 = (bf16[1,768,10,129]{1,3,2,0:T(8,128)(2,1)}, bf16[1,768,10,129]{1,3,2,0:T(8,128)(2,1)S(1)}, u32[]{:S(2)}) copy-start(bf16[1,768,10,129]{1,3,2,0:T(8,128)(2,1)S(1)} %get-tuple-element.59) | copy-start | bytes 5944324
  32.6 7.3 %copy-start.3 = (bf16[1,768,10,129]{1,3,2,0:T(8,128)(2,1)}, bf16[1,768,10,129]{1,3,2,0:T(8,128)(2,1)S(1)}, u32[]{:S(2)}) copy-start(bf16[1,768,10,129]{1,3,2,0:T(8,128)(2,1)S(1)} %get-tuple-element.60) | copy-start | bytes 5944324
  32.6 21.9 %copy-start.16 = (f32[768,48]{0,1:T(8,128)S(1)}, f32[768,48]{0,1:T(8,128)}, u32[]{:S(2)}) copy-start(f32[768,48]{0,1:T(8,128)} %param.12) | copy-start | bytes 442372
  32.7 22.1 %copy-start.15 = (f32[48,768]{1,0:T(8,128)S(1)}, f32[48,768]{1,0:T(8,128)}, u32[]{:S(2)}) copy-start(f32[48,768]{1,0:T(8,128)} %param.13) | copy-start | bytes 442372
  32.7 22.4 %copy-start.13 = (bf16[1,192,8,128]{3,2,1,0:T(8,128)(2,1)S(1)}, bf16[1,192,8,128]{3,2,1,0:T(8,128)(2,1)}, u32[]{:S(2)}) copy-start(bf16[1,192,8,128]{3,2,1,0:T(8,128)(2,1)} %param.8) | copy-start | bytes 1179652
  55.0 3.9 %copy-start.6 = (f32[1,768,8,128]{1,3,2,0:T(8,128)S(1)}, f32[1,768,8,128]{1,3,2,0:T(8,128)}, u32[]{:S(2)}) copy-start(f32[1,768,8,128]{1,3,2,0:T(8,128)} %get-tuple-element.54) | copy-start | bytes 9437188
  59.0 2.5 copy-start.2
  59.0 2.5 copy-start.4
  59.0 3.4 %copy-start.7 = (f32[768,8,128]{0,2,1:T(8,128)S(1)}, f32[768,8,128]{0,2,1:T(8,128)}, u32[]{:S(2)}) copy-start(f32[768,8,128]{0,2,1:T(8,128)} %get-tuple-element.71) | copy-start | bytes 9437188
  59.0 3.4 %copy-start.9 = (bf16[1,768,1,128]{1,3,2,0:T(8,128)(2,1)S(1)}, bf16[1,768,1,128]{1,3,2,0:T(8,128)(2,1)}, u32[]{:S(2)}) copy-start(bf16[1,768,1,128]{1,3,2,0:T(8,128)(2,1)} %copy-done.8) | copy-start | bytes 589828
  59.0 3.4 %copy-start.11 = (bf16[1,768,1,128]{1,3,2,0:T(8,128)(2,1)S(1)}, bf16[1,768,1,128]{1,3,2,0:T(8,128)(2,1)}, u32[]{:S(2)}) copy-start(bf16[1,768,1,128]{1,3,2,0:T(8,128)(2,1)} %copy-done.10) | copy-start | bytes 589828
  67.9 14.8 %copy-start.19 = (bf16[1,192,8,128]{3,1,2,0:T(8,128)(2,1)S(1)}, bf16[1,192,8,128]{3,1,2,0:T(8,128)(2,1)}, u32[]{:S(2)}) copy-start(bf16[1,192,8,128]{3,1,2,0:T(8,128)(2,1)} %fusion.46) | copy-start | bytes 1179652
  68.0 5.1 %collective-permute-start.4 = (bf16[1,768,1,128]{1,3,2,0:T(8,128)(2,1)S(1)}, bf16[1,768,1,128]{1,3,2,0:T(8,128)(2,1)S(1)}, u32[]{:S(2)}, u32[]{:S(2)}) collective-permute-start(bf16[1,768,1,128]{1,3,2,0:T(8,128)(2,1)S(1)} %get-tuple-element.63), channel_id=1, source_target_pairs={{0,4},{1,5},{2,6},{3,7},{8,12},{9,13},{10,14},{11,15},{16,20},{17,... | collective-permute-start | bytes 589832 | tf_op jit(solution)/shard_map/ppermute | solution.py:17
  69.9 7.6 %collective-permute-start.5 = (bf16[1,768,1,128]{1,3,2,0:T(8,128)(2,1)S(1)}, bf16[1,768,1,128]{1,3,2,0:T(8,128)(2,1)S(1)}, u32[]{:S(2)}, u32[]{:S(2)}) collective-permute-start(bf16[1,768,1,128]{1,3,2,0:T(8,128)(2,1)S(1)} %get-tuple-element.64), channel_id=1, source_target_pairs={{4,0},{5,1},{6,2},{7,3},{12,8},{13,9},{14,10},{15,11},{20,16},{21,... | collective-permute-start | bytes 589832 | tf_op jit(solution)/shard_map/ppermute | solution.py:18
  77.6 6.5 %collective-permute-start.6 = (bf16[1,768,10,1]{1,3,2,0:T(2,128)(2,1)S(1)}, bf16[1,768,10,1]{1,3,2,0:T(2,128)(2,1)S(1)}, u32[]{:S(2)}, u32[]{:S(2)}) collective-permute-start(bf16[1,768,10,1]{1,3,2,0:T(2,128)(2,1)S(1)} %get-tuple-element.57), channel_id=1, source_target_pairs={{1,0},{2,1},{3,2},{5,4},{6,5},{7,6},{9,8},{10,9},{11,10},{13,12},{... | collective-permute-start | bytes 46088 | tf_op jit(solution)/shard_map/ppermute | solution.py:18
  78.9 5.2 %collective-permute-start.7 = (bf16[1,768,10,1]{1,3,2,0:T(2,128)(2,1)S(1)}, bf16[1,768,10,1]{1,3,2,0:T(2,128)(2,1)S(1)}, u32[]{:S(2)}, u32[]{:S(2)}) collective-permute-start(bf16[1,768,10,1]{1,3,2,0:T(2,128)(2,1)S(1)} %get-tuple-element.58), channel_id=1, source_target_pairs={{0,1},{1,2},{2,3},{4,5},{5,6},{6,7},{8,9},{9,10},{10,11},{12,13},{... | collective-permute-start | bytes 46088 | tf_op jit(solution)/shard_map/ppermute | solution.py:17
  83.8 173.6 %all-reduce.7.cloned.1.call-start = ((), (), s32[]{:S(2)}) async-start(), calls=%async_computation | async-start | bytes 2359296 | tf_op jit(solution)/shard_map/psum | solution.py:112
  84.1 1.9 copy-start.5
  85.9 5.9 %copy-start.14 = (bf16[1,192,8,128]{3,2,1,0:T(8,128)(2,1)S(1)}, bf16[1,192,8,128]{3,2,1,0:T(8,128)(2,1)}, u32[]{:S(2)}) copy-start(bf16[1,192,8,128]{3,2,1,0:T(8,128)(2,1)} %param.8) | copy-start | bytes 1179652
  85.9 5.9 %copy-start.21 = (f32[192]{0:T(256)S(1)}, f32[192]{0:T(256)}, u32[]{:S(2)}) copy-start(f32[192]{0:T(256)} %param.9) | copy-start | bytes 2308
  91.9 1.4 copy-start.22
  91.9 3.6 %copy-start.18 = (bf16[1,192,8,128]{3,2,1,0:T(8,128)(2,1)S(1)}, bf16[1,192,8,128]{3,2,1,0:T(8,128)(2,1)}, u32[]{:S(2)}) copy-start(bf16[1,192,8,128]{3,2,1,0:T(8,128)(2,1)} %param.15) | copy-start | bytes 1179652
  (1 other events, 1.2 us)
Sparse Core Ops, SparseCore 0:
  83.9 36.2 all-reduce.8
  126.3 131.0 all-reduce.6
where the time goes:
time: 272 us; the launch traced here: 271 us
  waiting for transfers between devices  136 us (50%)
  blocking collectives  55.6 us (20%)
  matrix products  21.3 us (8%)
  starting transfers between devices  16.7 us (6%)
  other arithmetic  15.1 us (6%)
  between operations  14.5 us (5%)
  local copies, waits for them, and re-layouts  12.4 us (5%)
    psum x1, waiting for transfers between devices, local(): lax.psum((grad_gain, grad_wexp, grad_kernel, grad_project), ('dp', 'row',...  120 us
    psum x1, blocking collectives, local(): lax.psum((grad_gain, grad_wexp, grad_kernel, grad_project), ('dp', 'row',...  41 us
    psum x1, blocking collectives, local(): pooled = lax.psum(jnp.sum(act, axis=(2, 3)), ('row', 'col')) / pixels  14.6 us
    unnamed x52, local copies, waits for them, and re-layouts  12.1 us
    ppermute x4, waiting for transfers between devices, with_halo(): after = lax.ppermute(leading, axis, down)  12 us
    ppermute x4, starting transfers between devices, with_halo(): before = lax.ppermute(last, axis, up)  11.1 us
    dot_general x1, matrix products, local(): jnp.einsum('bchw,ec->behw', cotangent, w_project, preferred_element_type=...  7.21 us
    reduce_sum x1, other arithmetic, local(): jnp.sum(grad_conv.astype(jnp.float32) * hidden_pad[:, :, drow:drow + rows...  5.59 us
  transfers between devices with their start and end apart: 10, of which 6 were waited for; matrix products, arithmetic and copies ran while one was open for 5% of the time, Pallas kernels for 0%

commit v1 on v0

--- a/solution.py
+++ b/solution.py
@@ -1,10 +1,120 @@
 import jax
 import jax.numpy as jnp
 from jax import lax
+from jax.experimental import pallas as pl
+from jax.experimental.pallas import tpu as pltpu
 from jax.sharding import PartitionSpec as P
 
 EPS = 1e-06
 HIGH = lax.Precision.HIGHEST
+
+MESH = pl.DeviceIdType.MESH
+
+def sum_kernel(v_ref, out_ref, mate_buf, acc1, group_buf, acc2, deep_buf, send, recv):
+    groups, deep = v_ref.shape[1], v_ref.shape[2]
+    half_cols = lax.axis_size("col") // 2
+    d, w, c = (lax.axis_index(a) for a in ("dp", "row", "col"))
+    core = lax.rem(c, 2)
+    g = w * half_cols + c // 2
+
+    def mate():
+        return (d, w, c + 1 - 2 * core)
+
+    def peer(s):
+        at = lax.rem(g + s, groups)
+        return at, (d, at // half_cols, lax.rem(at, half_cols) * 2 + core)
+
+    def layer(s):
+        at = lax.rem(d + s, deep)
+        return at, (at, w, c)
+
+    barrier = pltpu.get_barrier_semaphore()
+    others = [mate()] + [peer(s)[1] for s in range(1, groups)]
+    others += [layer(s)[1] for s in range(1, deep)]
+    for other in others:
+        pl.semaphore_signal(barrier, inc=1, device_id=other, device_id_type=MESH)
+    pl.semaphore_wait(barrier, len(others))
+
+    def copy(src, dst, n, to):
+        return pltpu.make_async_remote_copy(
+            src_ref=src,
+            dst_ref=dst,
+            send_sem=send.at[n],
+            recv_sem=recv.at[n],
+            device_id=to,
+            device_id_type=MESH,
+        )
+
+    def run(copies):
+        for one in copies:
+            one.start()
+        for one in copies:
+            one.wait()
+
+    run([copy(v_ref.at[1 - core], mate_buf, 0, mate())])
+    acc1[...] = v_ref[core] + mate_buf[...]
+    n = 0
+    moves = []
+    for s in range(1, groups):
+        at, to = peer(s)
+        moves.append(copy(acc1.at[at], group_buf.at[s - 1], n + s, to))
+    run(moves)
+    part = acc1[g]
+    for s in range(1, groups):
+        part = part + group_buf[s - 1]
+    acc2[...] = part
+    n += groups - 1
+    moves = []
+    for s in range(1, deep):
+        at, to = layer(s)
+        moves.append(copy(acc2.at[at], deep_buf.at[s - 1], n + s, to))
+    run(moves)
+    part = acc2[d]
+    for s in range(1, deep):
+        part = part + deep_buf[s - 1]
+    out_ref[core, g, d] = part
+    n += deep - 1
+    mine = out_ref.at[core, g, d]
+    run([copy(mine, mine, n + s, layer(s)[1]) for s in range(1, deep)])
+    n += deep - 1
+    mine = out_ref.at[core, g]
+    run([copy(mine, mine, n + s, peer(s)[1]) for s in range(1, groups)])
+    n += groups
+    mine = out_ref.at[core]
+    run([copy(mine, mine, n, mate())])
+
+
+def sum_all(values):
+    rows, cols = values.shape
+    groups = lax.axis_size("row") * (lax.axis_size("col") // 2)
+    deep = lax.axis_size("dp")
+    each = -(-rows // (2 * groups * deep))
+    wide = -(-cols // 128) * 128
+    full = 2 * groups * deep * each
+    laid = jnp.pad(values, ((0, full - rows), (0, wide - cols)))
+    laid = laid.reshape(2, groups, deep, each, wide)
+    f32 = jnp.float32
+    count = 2 * (1 + groups - 1 + deep - 1) + 1
+    total = pl.pallas_call(
+        sum_kernel,
+        out_shape=jax.ShapeDtypeStruct(laid.shape, f32),
+        in_specs=[pl.BlockSpec(memory_space=pltpu.VMEM)],
+        out_specs=pl.BlockSpec(memory_space=pltpu.VMEM),
+        scratch_shapes=[
+            pltpu.VMEM((groups, deep, each, wide), f32),
+            pltpu.VMEM((groups, deep, each, wide), f32),
+            pltpu.VMEM((max(groups - 1, 1), deep, each, wide), f32),
+            pltpu.VMEM((deep, each, wide), f32),
+            pltpu.VMEM((max(deep - 1, 1), each, wide), f32),
+            pltpu.SemaphoreType.DMA((count,)),
+            pltpu.SemaphoreType.DMA((count,)),
+        ],
+        compiler_params=pltpu.CompilerParams(
+            collective_id=0, has_side_effects=True, vmem_limit_bytes=48 << 20
+        ),
+        name="sum_grads",
+    )(laid)
+    return total.reshape(full, wide)[:rows, :cols]
 
 
 def with_halo(shard, sides, width):
@@ -108,10 +218,23 @@
     grad_in = inverse * (
         grad_normed - normed * jnp.mean(grad_normed * normed, axis=1, keepdims=True)
     ) + cotangent.astype(jnp.float32)
-    grad_wsq_all, grad_wexc_all = lax.psum((grad_wsq, grad_wexc), "dp")
-    gain_all, wexp_all, kernel_all, project_all = lax.psum(
-        (grad_gain, grad_wexp, grad_kernel, grad_project), ("dp", "row", "col")
-    )
+    lead = jnp.logical_and(lax.axis_index("row") == 0, lax.axis_index("col") == 0)
+    keep = lead.astype(jnp.float32)
+    hidden_n = grad_project.shape[0]
+    pieces = [
+        grad_project,
+        grad_wexp.T,
+        grad_kernel,
+        grad_wsq * keep,
+        grad_wexc.T * keep,
+        jnp.pad(grad_gain, (0, hidden_n - chans))[:, None],
+    ]
+    sizes = [p.shape[1] for p in pieces]
+    total = sum_all(jnp.concatenate(pieces, axis=1))
+    ends = [sum(sizes[: n + 1]) for n in range(len(sizes))]
+    parts = [total[:, e - n : e] for e, n in zip(ends, sizes)]
+    project_all, wexp_all, kernel_all = parts[0], parts[1].T, parts[2]
+    grad_wsq_all, grad_wexc_all, gain_all = parts[3], parts[4].T, parts[5][:chans, 0]
     return (
         output,
         grad_in.astype(jnp.bfloat16),

time: 272 us -> 131 us (0.48)
  waiting for transfers between devices: 136 us -> 15.5 us
  blocking collectives: 55.6 us -> 14.6 us
  Pallas kernels: 0 us -> 37.9 us
  between operations: 14.5 us -> 1.21 us
  matrix products: 21.3 us -> 18.2 us
    psum x2 -> x0, waiting for transfers between devices: 120 us -> none  [the longest x1 120 us: local(): lax.psum((grad_gain, grad_wexp, grad_kernel, grad_project), ('dp', 'row',...]
    psum x1 -> x0, blocking collectives: 41 us -> none  [local(): lax.psum((grad_gain, grad_wexp, grad_kernel, grad_project), ('dp', 'row',...]
    pallas_call x0 -> x1, Pallas kernels: none -> 37.9 us  [sum_all(): pl.pallas_call(sum_kernel, out_shape=jax.ShapeDtypeStruct(laid.shape, f32...]
    unnamed x52 -> x45, local copies, waits for them, and re-layouts: 12.1 us -> 11.1 us
  transfers between devices with their start and end apart: 10 -> 8, of which waited for: 6 -> 5; matrix products, arithmetic and copies ran while one was open for 5% -> 2% of each run, Pallas kernels for 0% -> 0%
where the time goes in v1:
time: 131 us
  Pallas kernels  37.9 us (29%)
  matrix products  18.2 us (14%)
  starting transfers between devices  16.5 us (13%)
  waiting for transfers between devices  15.5 us (12%)
  blocking collectives  14.6 us (11%)
  other arithmetic  13.7 us (10%)
  local copies, waits for them, and re-layouts  12.9 us (10%)
    pallas_call x1, Pallas kernels, sum_all(): pl.pallas_call(sum_kernel, out_shape=jax.ShapeDtypeStruct(laid.shape, f32...  37.9 us
    psum x1, blocking collectives, local(): pooled = lax.psum(jnp.sum(act, axis=(2, 3)), ('row', 'col')) / pixels  14.6 us
    ppermute x4, waiting for transfers between devices, with_halo(): after = lax.ppermute(leading, axis, down)  12 us
    ppermute x4, starting transfers between devices, with_halo(): before = lax.ppermute(last, axis, up)  11.2 us
    unnamed x45, local copies, waits for them, and re-layouts  11.1 us
    dot_general x1, matrix products, local(): jnp.einsum('bchw,ec->behw', cotangent, w_project, preferred_element_type=...  7.2 us
    reduce_sum x1, other arithmetic, local(): jnp.sum(grad_conv.astype(jnp.float32) * hidden_pad[:, :, drow:drow + rows...  5.57 us
    ppermute x4, starting transfers between devices, with_halo(): after = lax.ppermute(leading, axis, down)  5.3 us
  transfers between devices with their start and end apart: 8, of which 5 were waited for; matrix products, arithmetic and copies ran while one was open for 2% of the time, Pallas kernels for 0%

profile of v1, /device:TPU:0, one launch (start us, length us, event | category | flops | bytes accessed | tf_op | source)
XLA Modules:
  0.0 130.5 jit_solution(4297720171702436222)
XLA Ops:
  0.6 1.1 fusion.59
  1.8 3.8 %fusion.30 = (bf16[768,8,128]{0,2,1:T(8,128)(2,1)S(1)}, f32[8,128,768]{2,1,0:T(8,128)}) fusion(bf16[192,768]{1,0:T(8,128)(2,1)} %param.10, f32[192]{0:T(256)} %param.9, f32[8,128]{1,0:T(8,128)S(1)} %add_rsqrt_fusion, bf16[1,192,8,128]{3,2,1,0:T(8,128)(2,1)} %param.8), kind=kOutput, calls=%fused_computation.55 | convolution fusion | flops 306708480 | bytes 5411584 | tf_op jit(solution)/shard_map/bchw,ce->behw/dot_general | solution.py:147
  5.6 4.9 %collective-permute-start = (bf16[1,768,1,128]{1,3,2,0:T(8,128)(2,1)S(1)}, bf16[1,768,1,128]{1,3,2,0:T(8,128)(2,1)S(1)}, u32[]{:S(2)}, u32[]{:S(2)}) collective-permute-start(bf16[1,768,1,128]{1,3,2,0:T(8,128)(2,1)S(1)} %get-tuple-element.71), channel_id=1, source_target_pairs={{0,4},{1,5},{2,6},{3,7},{8,12},{9,13},{10,14},{11,15},{16,20},{17,... | collective-permute-start | bytes 589832 | tf_op jit(solution)/shard_map/ppermute | solution.py:127
  10.5 1.3 collective-permute-start.1
  11.8 2.8 %collective-permute-done = bf16[1,768,1,128]{1,3,2,0:T(8,128)(2,1)S(1)} collective-permute-done((bf16[1,768,1,128]{1,3,2,0:T(8,128)(2,1)S(1)}, bf16[1,768,1,128]{1,3,2,0:T(8,128)(2,1)S(1)}, u32[]{:S(2)}, u32[]{:S(2)}) %collective-permute-start) | collective-permute-done | bytes 196640 | tf_op jit(solution)/shard_map/ppermute | solution.py:127
  14.6 4.1 %collective-permute-done.1 = bf16[1,768,1,128]{1,3,2,0:T(8,128)(2,1)S(1)} collective-permute-done((bf16[1,768,1,128]{1,3,2,0:T(8,128)(2,1)S(1)}, bf16[1,768,1,128]{1,3,2,0:T(8,128)(2,1)S(1)}, u32[]{:S(2)}, u32[]{:S(2)}) %collective-permute-start.1) | collective-permute-done | bytes 196640 | tf_op jit(solution)/shard_map/ppermute | solution.py:128
  18.8 1.3 collective-permute-start.2
  20.1 1.4 %collective-permute-start.3 = (bf16[1,768,10,1]{1,3,2,0:T(2,128)(2,1)S(1)}, bf16[1,768,10,1]{1,3,2,0:T(2,128)(2,1)S(1)}, u32[]{:S(2)}, u32[]{:S(2)}) collective-permute-start(bf16[1,768,10,1]{1,3,2,0:T(2,128)(2,1)S(1)} %get-tuple-element.64), channel_id=1, source_target_pairs={{1,0},{2,1},{3,2},{5,4},{6,5},{7,6},{9,8},{10,9},{11,10},{13,12},{... | collective-permute-start | bytes 46088 | tf_op jit(solution)/shard_map/ppermute | solution.py:128
  21.7 3.4 %collective-permute-done.3 = bf16[1,768,10,1]{1,3,2,0:T(2,128)(2,1)S(1)} collective-permute-done((bf16[1,768,10,1]{1,3,2,0:T(2,128)(2,1)S(1)}, bf16[1,768,10,1]{1,3,2,0:T(2,128)(2,1)S(1)}, u32[]{:S(2)}, u32[]{:S(2)}) %collective-permute-start.3) | collective-permute-done | bytes 15392 | tf_op jit(solution)/shard_map/ppermute | solution.py:128
  25.1 0.9 maximum_maximum_fusion
  26.1 7.2 %fusion.26 = (f32[768]{0:T(1024)S(1)}, f32[768]{0:T(1024)S(1)}, f32[1,768,8,128]{1,3,2,0:T(8,128)}, f32[768,8,128]{0,2,1:T(8,128)}) fusion(bf16[1,768,10,129]{1,3,2,0:T(8,128)(2,1)S(1)} %get-tuple-element.62, f32[768]{0:T(1024)S(1)} %get-tuple-element.49, bf16[1,768,1,128]{1,3,2,0:T(8,128)(2,1)S(1)} %collective-permute-done.1, ...), kind=kOutput, calls=%fused_computation.48 | convolution fusion | flops 329513472 | bytes 19989504 | tf_op jit(solution)/shard_map/bchw,ec->behw/dot_general | solution.py:179
  33.3 14.6 %all-reduce.2 = (f32[1,768]{1,0:T(1,128)S(1)}, f32[1,768]{1,0:T(1,128)S(1)}) all-reduce(f32[1,768]{1,0:T(1,128)S(1)} %reduce_sum.132, f32[1,768]{1,0:T(1,128)S(1)} %reduce_sum.134), channel_id=1, replica_groups=mesh['dp'=4,'row'=2,'col'=4] {'row','col'}, use_global_device_ids=true, to_apply=%region_2.3 | all-reduce | flops 1536 | bytes 12288 | tf_op jit(solution)/shard_map/psum | solution.py:171
  49.0 3.2 %fusion.46 = bf16[1,192,8,128]{3,1,2,0:T(8,128)(2,1)S(1)} fusion(f32[768]{0:T(1024)S(1)} %get-tuple-element.74, bf16[768,192]{0,1:T(8,128)(2,1)S(1)} %copy-done, bf16[1,192,8,128]{3,2,1,0:T(8,128)(2,1)S(1)} %copy-done.8, f32[1,768,8,128]{1,3,2,0:T(8,128)} %get-tuple-element.56), kind=kOutput, calls=%fused_computation.79 | convolution fusion | flops 307298304 | bytes 4230144 | tf_op jit(solution)/shard_map/behw,ec->bchw/dot_general | solution.py:177
  52.2 0.9 copy-done.6
  53.1 0.9 copy-done.7
  53.9 5.6 %fusion.24 = (f32[768]{0:T(1024)S(1)}, f32[768]{0:T(1024)S(1)}, f32[768]{0:T(1024)S(1)}, f32[768]{0:T(1024)S(1)}, f32[768]{0:T(1024)S(1)}, /*index=5*/f32[768]{0...) fusion(bf16[1,768,10,129]{1,3,2,0:T(8,128)(2,1)S(1)} %copy-done.4, ...), kind=kLoop, calls=%fused_computation.44 | loop fusion | flops 32236800 | bytes 20874240 | tf_op jit(solution)/shard_map/reduce_sum | solution.py:204
  59.6 1.8 %collective-permute-start.4 = (bf16[1,768,1,128]{1,3,2,0:T(8,128)(2,1)S(1)}, bf16[1,768,1,128]{1,3,2,0:T(8,128)(2,1)S(1)}, u32[]{:S(2)}, u32[]{:S(2)}) collective-permute-start(bf16[1,768,1,128]{1,3,2,0:T(8,128)(2,1)S(1)} %get-tuple-element.69), channel_id=1, source_target_pairs={{0,4},{1,5},{2,6},{3,7},{8,12},{9,13},{10,14},{11,15},{16,20},{17,... | collective-permute-start | bytes 589832 | tf_op jit(solution)/shard_map/ppermute | solution.py:127
  61.4 1.3 collective-permute-start.5
  62.7 1.1 convolution_bitcast_fusion.1
  64.5 4.4 %collective-permute-done.5 = bf16[1,768,1,128]{1,3,2,0:T(8,128)(2,1)S(1)} collective-permute-done((bf16[1,768,1,128]{1,3,2,0:T(8,128)(2,1)S(1)}, bf16[1,768,1,128]{1,3,2,0:T(8,128)(2,1)S(1)}, u32[]{:S(2)}, u32[]{:S(2)}) %collective-permute-start.5) | collective-permute-done | bytes 196640 | tf_op jit(solution)/shard_map/ppermute | solution.py:128
  69.0 1.3 collective-permute-start.6
  70.3 3.2 %collective-permute-start.7 = (bf16[1,768,10,1]{1,3,2,0:T(2,128)(2,1)S(1)}, bf16[1,768,10,1]{1,3,2,0:T(2,128)(2,1)S(1)}, u32[]{:S(2)}, u32[]{:S(2)}) collective-permute-start(bf16[1,768,10,1]{1,3,2,0:T(2,128)(2,1)S(1)} %get-tuple-element.60), channel_id=1, source_target_pairs={{0,1},{1,2},{2,3},{4,5},{5,6},{6,7},{8,9},{9,10},{10,11},{12,13},{... | collective-permute-start | bytes 46088 | tf_op jit(solution)/shard_map/ppermute | solution.py:127
  73.7 1.0 copy.47
  74.7 0.9 pad_maximum_fusion.1
  75.7 1.0 copy-done.5
  76.6 4.7 %fusion.15 = bf16[1,768,8,128]{1,3,2,0:T(8,128)(2,1)S(1)} fusion(bf16[1,768,8,128]{1,3,2,0:T(8,128)(2,1)S(1)} %get-tuple-element.55, f32[8,128,768]{2,1,0:T(8,128)S(1)} %copy-done.5, bf16[1,768,10,129]{1,3,2,0:T(8,128)(2,1)S(1)} %get-tuple-element.58, bf16[1,768,1,128]{1,3,2,0:T(8,128)(2,1)S(1)} %collective-permute-done.4, ...), kind=kLoop, calls=%fused_computation.35 | loop fusion | flops 29097984 | bytes 16149504 | tf_op jit(solution)/shard_map/convert_element_type | solution.py:211
  81.9 1.6 %fusion.58 = (f32[192]{0:T(256)S(1)}, f32[8,128]{1,0:T(8,128)S(1)}, f32[1,192,8,128]{3,1,2,0:T(8,128)}) fusion(f32[8,128]{1,0:T(8,128)S(1)} %add_rsqrt_fusion, bf16[1,192,8,128]{3,2,1,0:T(8,128)(2,1)S(1)} %copy-done.8, f32[192]{0:T(256)S(1)} %copy-done.16, bf16[192,768]{1,0:T(8,128)(2,1)S(1)} %copy-done.17, bf16[1,768,8,128]{1,3,2,0:T(8,128)(2,1)S(1)} %fusion.15), kind=kOutput, calls=%fused_computation.97 | convolution fusion | flops 303364928 | bytes 3057152 | tf_op jit(solution)/shard_map/ce,behw->bchw/dot_general | solution.py:213
  84.9 37.9 %sum_grads.1 = f32[2,4,4,24,512]{4,3,2,1,0:T(8,128)S(1)} custom-call(f32[2,4,4,24,512]{4,3,2,1,0:T(8,128)S(1)} %bitcast.132), custom_call_target="tpu_custom_call" | custom-call | tf_op jit(solution)/shard_map/sum_grads/pallas_call | solution.py:98
  124.3 1.0 copy.48
  126.8 0.8 copy.57
  127.6 1.1 copy.58
  129.4 1.1 copy.54
  (78 shorter events, 7.8 us)
Async XLA Ops:
  0.6 25.4 %copy-start = (bf16[768,192]{0,1:T(8,128)(2,1)S(1)}, bf16[768,192]{0,1:T(8,128)(2,1)}, u32[]{:S(2)}) copy-start(bf16[768,192]{0,1:T(8,128)(2,1)} %param.14) | copy-start | bytes 884740
  1.8 19.8 %copy-start.15 = (f32[768,9]{0,1:T(8,128)S(1)}, f32[768,9]{0,1:T(8,128)}, u32[]{:S(2)}) copy-start(f32[768,9]{0,1:T(8,128)} %param.11) | copy-start | bytes 82948
  5.6 9.0 %collective-permute-start = (bf16[1,768,1,128]{1,3,2,0:T(8,128)(2,1)S(1)}, bf16[1,768,1,128]{1,3,2,0:T(8,128)(2,1)S(1)}, u32[]{:S(2)}, u32[]{:S(2)}) collective-permute-start(bf16[1,768,1,128]{1,3,2,0:T(8,128)(2,1)S(1)} %get-tuple-element.71), channel_id=1, source_target_pairs={{0,4},{1,5},{2,6},{3,7},{8,12},{9,13},{10,14},{11,15},{16,20},{17,... | collective-permute-start | bytes 589832 | tf_op jit(solution)/shard_map/ppermute | solution.py:127
  10.5 8.3 %collective-permute-start.1 = (bf16[1,768,1,128]{1,3,2,0:T(8,128)(2,1)S(1)}, bf16[1,768,1,128]{1,3,2,0:T(8,128)(2,1)S(1)}, u32[]{:S(2)}, u32[]{:S(2)}) collective-permute-start(bf16[1,768,1,128]{1,3,2,0:T(8,128)(2,1)S(1)} %get-tuple-element.72), channel_id=1, source_target_pairs={{4,0},{5,1},{6,2},{7,3},{12,8},{13,9},{14,10},{15,11},{20,16},{21,... | collective-permute-start | bytes 589832 | tf_op jit(solution)/shard_map/ppermute | solution.py:128
  18.8 2.9 %collective-permute-start.2 = (bf16[1,768,10,1]{1,3,2,0:T(2,128)(2,1)S(1)}, bf16[1,768,10,1]{1,3,2,0:T(2,128)(2,1)S(1)}, u32[]{:S(2)}, u32[]{:S(2)}) collective-permute-start(bf16[1,768,10,1]{1,3,2,0:T(2,128)(2,1)S(1)} %get-tuple-element.63), channel_id=1, source_target_pairs={{0,1},{1,2},{2,3},{4,5},{5,6},{6,7},{8,9},{9,10},{10,11},{12,13},{... | collective-permute-start | bytes 46088 | tf_op jit(solution)/shard_map/ppermute | solution.py:127
  20.1 5.9 %copy-start.13 = (bf16[1,192,8,128]{3,2,1,0:T(8,128)(2,1)S(1)}, bf16[1,192,8,128]{3,2,1,0:T(8,128)(2,1)}, u32[]{:S(2)}) copy-start(bf16[1,192,8,128]{3,2,1,0:T(8,128)(2,1)} %param.15) | copy-start | bytes 1179652
  20.1 5.0 %collective-permute-start.3 = (bf16[1,768,10,1]{1,3,2,0:T(2,128)(2,1)S(1)}, bf16[1,768,10,1]{1,3,2,0:T(2,128)(2,1)S(1)}, u32[]{:S(2)}, u32[]{:S(2)}) collective-permute-start(bf16[1,768,10,1]{1,3,2,0:T(2,128)(2,1)S(1)} %get-tuple-element.64), channel_id=1, source_target_pairs={{1,0},{2,1},{3,2},{5,4},{6,5},{7,6},{9,8},{10,9},{11,10},{13,12},{... | collective-permute-start | bytes 46088 | tf_op jit(solution)/shard_map/ppermute | solution.py:128
  26.0 7.3 %copy-start.1 = (bf16[1,768,10,129]{1,3,2,0:T(8,128)(2,1)}, bf16[1,768,10,129]{1,3,2,0:T(8,128)(2,1)S(1)}, u32[]{:S(2)}) copy-start(bf16[1,768,10,129]{1,3,2,0:T(8,128)(2,1)S(1)} %get-tuple-element.61) | copy-start | bytes 5944324
  26.0 7.3 %copy-start.3 = (bf16[1,768,10,129]{1,3,2,0:T(8,128)(2,1)}, bf16[1,768,10,129]{1,3,2,0:T(8,128)(2,1)S(1)}, u32[]{:S(2)}) copy-start(bf16[1,768,10,129]{1,3,2,0:T(8,128)(2,1)S(1)} %get-tuple-element.62) | copy-start | bytes 5944324
  26.1 21.9 %copy-start.12 = (f32[768,48]{0,1:T(8,128)S(1)}, f32[768,48]{0,1:T(8,128)}, u32[]{:S(2)}) copy-start(f32[768,48]{0,1:T(8,128)} %param.12) | copy-start | bytes 442372
  26.1 22.1 %copy-start.11 = (f32[48,768]{1,0:T(8,128)S(1)}, f32[48,768]{1,0:T(8,128)}, u32[]{:S(2)}) copy-start(f32[48,768]{1,0:T(8,128)} %param.13) | copy-start | bytes 442372
  26.1 22.9 %copy-start.8 = (bf16[1,192,8,128]{3,2,1,0:T(8,128)(2,1)S(1)}, bf16[1,192,8,128]{3,2,1,0:T(8,128)(2,1)}, u32[]{:S(2)}) copy-start(bf16[1,192,8,128]{3,2,1,0:T(8,128)(2,1)} %param.8) | copy-start | bytes 1179652
  48.9 3.2 %copy-start.2 = (bf16[1,768,10,129]{1,3,2,0:T(8,128)(2,1)S(1)}, bf16[1,768,10,129]{1,3,2,0:T(8,128)(2,1)}, u32[]{:S(2)}) copy-start(bf16[1,768,10,129]{1,3,2,0:T(8,128)(2,1)} %copy-done.1) | copy-start | bytes 5944324
  49.0 3.2 %copy-start.4 = (bf16[1,768,10,129]{1,3,2,0:T(8,128)(2,1)S(1)}, bf16[1,768,10,129]{1,3,2,0:T(8,128)(2,1)}, u32[]{:S(2)}) copy-start(bf16[1,768,10,129]{1,3,2,0:T(8,128)(2,1)} %copy-done.3) | copy-start | bytes 5944324
  49.0 4.1 %copy-start.6 = (f32[1,768,8,128]{1,3,2,0:T(8,128)S(1)}, f32[1,768,8,128]{1,3,2,0:T(8,128)}, u32[]{:S(2)}) copy-start(f32[1,768,8,128]{1,3,2,0:T(8,128)} %get-tuple-element.56) | copy-start | bytes 9437188
  49.0 5.0 %copy-start.7 = (f32[768,8,128]{0,2,1:T(8,128)S(1)}, f32[768,8,128]{0,2,1:T(8,128)}, u32[]{:S(2)}) copy-start(f32[768,8,128]{0,2,1:T(8,128)} %get-tuple-element.77) | copy-start | bytes 9437188
  59.6 5.0 %collective-permute-start.4 = (bf16[1,768,1,128]{1,3,2,0:T(8,128)(2,1)S(1)}, bf16[1,768,1,128]{1,3,2,0:T(8,128)(2,1)S(1)}, u32[]{:S(2)}, u32[]{:S(2)}) collective-permute-start(bf16[1,768,1,128]{1,3,2,0:T(8,128)(2,1)S(1)} %get-tuple-element.69), channel_id=1, source_target_pairs={{0,4},{1,5},{2,6},{3,7},{8,12},{9,13},{10,14},{11,15},{16,20},{17,... | collective-permute-start | bytes 589832 | tf_op jit(solution)/shard_map/ppermute | solution.py:127
  61.4 7.6 %collective-permute-start.5 = (bf16[1,768,1,128]{1,3,2,0:T(8,128)(2,1)S(1)}, bf16[1,768,1,128]{1,3,2,0:T(8,128)(2,1)S(1)}, u32[]{:S(2)}, u32[]{:S(2)}) collective-permute-start(bf16[1,768,1,128]{1,3,2,0:T(8,128)(2,1)S(1)} %get-tuple-element.70), channel_id=1, source_target_pairs={{4,0},{5,1},{6,2},{7,3},{12,8},{13,9},{14,10},{15,11},{20,16},{21,... | collective-permute-start | bytes 589832 | tf_op jit(solution)/shard_map/ppermute | solution.py:128
  69.0 5.7 %collective-permute-start.6 = (bf16[1,768,10,1]{1,3,2,0:T(2,128)(2,1)S(1)}, bf16[1,768,10,1]{1,3,2,0:T(2,128)(2,1)S(1)}, u32[]{:S(2)}, u32[]{:S(2)}) collective-permute-start(bf16[1,768,10,1]{1,3,2,0:T(2,128)(2,1)S(1)} %get-tuple-element.59), channel_id=1, source_target_pairs={{1,0},{2,1},{3,2},{5,4},{6,5},{7,6},{9,8},{10,9},{11,10},{13,12},{... | collective-permute-start | bytes 46088 | tf_op jit(solution)/shard_map/ppermute | solution.py:128
  70.3 4.4 %collective-permute-start.7 = (bf16[1,768,10,1]{1,3,2,0:T(2,128)(2,1)S(1)}, bf16[1,768,10,1]{1,3,2,0:T(2,128)(2,1)S(1)}, u32[]{:S(2)}, u32[]{:S(2)}) collective-permute-start(bf16[1,768,10,1]{1,3,2,0:T(2,128)(2,1)S(1)} %get-tuple-element.60), channel_id=1, source_target_pairs={{0,1},{1,2},{2,3},{4,5},{5,6},{6,7},{8,9},{9,10},{10,11},{12,13},{... | collective-permute-start | bytes 46088 | tf_op jit(solution)/shard_map/ppermute | solution.py:127
  74.7 1.9 %copy-start.5 = (f32[8,128,768]{2,1,0:T(8,128)S(1)}, f32[8,128,768]{2,1,0:T(8,128)}, u32[]{:S(2)}) copy-start(f32[8,128,768]{2,1,0:T(8,128)} %get-tuple-element.76) | copy-start | bytes 9437188
  76.6 4.8 %copy-start.16 = (f32[192]{0:T(256)S(1)}, f32[192]{0:T(256)}, u32[]{:S(2)}) copy-start(f32[192]{0:T(256)} %param.9) | copy-start | bytes 2308
  76.6 5.3 %copy-start.17 = (bf16[192,768]{1,0:T(8,128)(2,1)S(1)}, bf16[192,768]{1,0:T(8,128)(2,1)}, u32[]{:S(2)}) copy-start(bf16[192,768]{1,0:T(8,128)(2,1)} %param.10) | copy-start | bytes 884740
  122.7 1.0 copy-start.9
  122.7 1.2 copy-start.10
  122.8 1.3 %copy-start.14 = (bf16[1,192,8,128]{3,2,1,0:T(8,128)(2,1)S(1)}, bf16[1,192,8,128]{3,2,1,0:T(8,128)(2,1)}, u32[]{:S(2)}) copy-start(bf16[1,192,8,128]{3,2,1,0:T(8,128)(2,1)} %param.15) | copy-start | bytes 1179652

commit v2 on v1

--- a/solution.py
+++ b/solution.py
@@ -117,17 +117,134 @@
     return total.reshape(full, wide)[:rows, :cols]
 
 
-def with_halo(shard, sides, width):
-    for axis, dim in sides:
-        count, length = (lax.axis_size(axis), shard.shape[dim])
-        up = [(i, (i + 1) % count) for i in range(count - 1)]
-        down = [(j, i) for i, j in up]
-        last = lax.slice_in_dim(shard, length - width, length, axis=dim)
-        leading = lax.slice_in_dim(shard, 0, width, axis=dim)
-        before = lax.ppermute(last, axis, up)
-        after = lax.ppermute(leading, axis, down)
-        shard = jnp.concatenate([before, shard, after], axis=dim)
-    return shard
+def greet(others):
+    barrier = pltpu.get_barrier_semaphore()
+    for other in others:
+        pl.semaphore_signal(barrier, inc=1, device_id=other, device_id_type=MESH)
+    pl.semaphore_wait(barrier, len(others))
+
+
+def halo_kernel(rows_ref, cols_ref, got_rows, got_cols, send, recv):
+    d, w, c = (lax.axis_index(a) for a in ("dp", "row", "col"))
+    count, wide = lax.axis_size("row"), lax.axis_size("col")
+
+    def at(drow, dcol):
+        return (d, lax.rem(w + drow + count, count), lax.rem(c + dcol + wide, wide))
+
+    plan = [
+        (rows_ref.at[1], got_rows.at[0], at(1, 0)),
+        (rows_ref.at[0], got_rows.at[1], at(-1, 0)),
+    ]
+    for side, dcol in enumerate((1, -1)):
+        for drow in (-1, 0, 1):
+            slot = got_cols.at[side * 3 + 1 - drow]
+            plan.append((cols_ref.at[1 - side], slot, at(drow, dcol)))
+    greet([to for _, _, to in plan])
+    copies = [
+        pltpu.make_async_remote_copy(
+            src_ref=src,
+            dst_ref=dst,
+            send_sem=send.at[n],
+            recv_sem=recv.at[n],
+            device_id=to,
+            device_id_type=MESH,
+        )
+        for n, (src, dst, to) in enumerate(plan)
+    ]
+    for copy in copies:
+        copy.start()
+    for copy in copies:
+        copy.wait()
+
+
+def with_halo(shard, number):
+    _, chans, rows, cols = shard.shape
+    count, wide = lax.axis_size("row"), lax.axis_size("col")
+    w, c = lax.axis_index("row"), lax.axis_index("col")
+    own = shard[0]
+    tall = -(-rows // 16) * 16
+    edge_rows = jnp.stack([own[:, 0, :], own[:, rows - 1, :]])
+    edge_cols = jnp.stack([own[:, :, 0].T, own[:, :, cols - 1].T])
+    edge_cols = jnp.pad(edge_cols, ((0, 0), (0, tall - rows), (0, 0)))
+    got_rows, got_cols = pl.pallas_call(
+        halo_kernel,
+        out_shape=[
+            jax.ShapeDtypeStruct(edge_rows.shape, shard.dtype),
+            jax.ShapeDtypeStruct((6, tall, chans), shard.dtype),
+        ],
+        in_specs=[pl.BlockSpec(memory_space=pltpu.VMEM)] * 2,
+        out_specs=[pl.BlockSpec(memory_space=pltpu.VMEM)] * 2,
+        scratch_shapes=[pltpu.SemaphoreType.DMA((8,)), pltpu.SemaphoreType.DMA((8,))],
+        compiler_params=pltpu.CompilerParams(
+            collective_id=number, has_side_effects=True, vmem_limit_bytes=48 << 20
+        ),
+        name="halo",
+    )(edge_rows, edge_cols)
+    up, down = w > 0, w < count - 1
+    zero = jnp.zeros((), shard.dtype)
+    above = jnp.where(up, got_rows[0], zero)[:, None, :]
+    below = jnp.where(down, got_rows[1], zero)[:, None, :]
+
+    def side(got, there):
+        top = jnp.where(up, got[0, rows - 1 : rows], zero)
+        bottom = jnp.where(down, got[2, 0:1], zero)
+        whole = jnp.concatenate([top, got[1, :rows], bottom], axis=0)
+        return jnp.where(there, whole, zero).T[:, :, None]
+
+    mid = jnp.concatenate([above, own, below], axis=1)
+    left, right = side(got_cols[:3], c > 0), side(got_cols[3:], c < wide - 1)
+    return jnp.concatenate([left, mid, right], axis=2)[None]
+
+
+def sample_kernel(v_ref, out_ref, buf, send, recv):
+    d, w, c = (lax.axis_index(a) for a in ("dp", "row", "col"))
+    wide = lax.axis_size("col")
+    group = lax.axis_size("row") * wide
+    me = w * wide + c
+    others = []
+    for s in range(1, group):
+        at = lax.rem(me + s, group)
+        others.append((d, at // wide, lax.rem(at, wide)))
+    greet(others)
+    copies = [
+        pltpu.make_async_remote_copy(
+            src_ref=v_ref,
+            dst_ref=buf.at[me],
+            send_sem=send.at[n],
+            recv_sem=recv.at[n],
+            device_id=to,
+            device_id_type=MESH,
+        )
+        for n, to in enumerate(others)
+    ]
+    for copy in copies:
+        copy.start()
+    buf[me] = v_ref[...]
+    for copy in copies:
+        copy.wait()
+    total = buf[0]
+    for s in range(1, group):
+        total = total + buf[s]
+    out_ref[...] = total
+
+
+def sample_sum(values):
+    group = lax.axis_size("row") * lax.axis_size("col")
+    return pl.pallas_call(
+        sample_kernel,
+        out_shape=jax.ShapeDtypeStruct(values.shape, values.dtype),
+        in_specs=[pl.BlockSpec(memory_space=pltpu.VMEM)],
+        out_specs=pl.BlockSpec(memory_space=pltpu.VMEM),
+        scratch_shapes=[
+            pltpu.VMEM((group, *values.shape), values.dtype),
+            pltpu.SemaphoreType.DMA((group - 1,)),
+            pltpu.SemaphoreType.DMA((group - 1,)),
+        ],
+        compiler_params=pltpu.CompilerParams(
+            collective_id=3, has_side_effects=True, vmem_limit_bytes=48 << 20
+        ),
+        name="sample_sum",
+    )(values)
 
 
 def silu_slope(value):
@@ -165,10 +282,16 @@
     normed, inverse, scaled = normalize(inputs, norm_gain)
     pre = expand(scaled, w_expand)
     hidden = jax.nn.silu(pre).astype(jnp.bfloat16)
-    hidden_pad = with_halo(hidden, (("row", 2), ("col", 3)), 1)
+    hidden_pad = with_halo(hidden, 1)
     conv = depthwise(hidden_pad, kernel, rows, cols)
     act = jax.nn.silu(conv)
-    pooled = lax.psum(jnp.sum(act, axis=(2, 3)), ("row", "col")) / pixels
+    grad_gated = jnp.einsum(
+        "bchw,ec->behw", cotangent, w_project, preferred_element_type=jnp.float32
+    )
+    sums = sample_sum(
+        jnp.concatenate([jnp.sum(act, axis=(2, 3)), jnp.sum(grad_gated * act, axis=(2, 3))])
+    )
+    pooled = sums[:batch] / pixels
     squeeze_pre = jnp.dot(pooled, w_squeeze, precision=HIGH)
     squeezed = jax.nn.silu(squeeze_pre)
     excite_pre = jnp.dot(squeezed, w_excite, precision=HIGH)
@@ -176,11 +299,8 @@
     gated = (act * excite[:, :, None, None]).astype(jnp.bfloat16)
     proj = jnp.einsum("behw,ec->bchw", gated, w_project, preferred_element_type=jnp.float32)
     output = (inputs.astype(jnp.float32) + proj).astype(jnp.bfloat16)
-    grad_gated = jnp.einsum(
-        "bchw,ec->behw", cotangent, w_project, preferred_element_type=jnp.float32
-    )
     grad_project = jnp.einsum("behw,bchw->ec", gated, cotangent, preferred_element_type=jnp.float32)
-    grad_excite = lax.psum(jnp.sum(grad_gated * act, axis=(2, 3)), ("row", "col"))
+    grad_excite = sums[batch:]
     grad_epre = grad_excite * excite * (1.0 - excite)
     grad_wexc = jnp.einsum("bs,be->se", squeezed, grad_epre, precision=HIGH)
     grad_spre = jnp.einsum("be,se->bs", grad_epre, w_excite, precision=HIGH) * silu_slope(
@@ -190,7 +310,7 @@
     grad_pooled = jnp.einsum("bs,es->be", grad_spre, w_squeeze, precision=HIGH)
     grad_act = grad_gated * excite[:, :, None, None] + (grad_pooled / pixels)[:, :, None, None]
     grad_conv = (grad_act * silu_slope(conv)).astype(jnp.bfloat16)
-    grad_pad = with_halo(grad_conv, (("row", 2), ("col", 3)), 1)
+    grad_pad = with_halo(grad_conv, 2)
     grad_hidden = jnp.zeros(pre.shape, jnp.float32)
     taps = []
     for tap in range(9):

time: 131 us -> 144 us (1.099)
  Pallas kernels: 37.9 us -> 72.2 us
  local copies, waits for them, and re-layouts: 12.9 us -> 32.1 us
  starting transfers between devices: 16.5 us -> 0 us
  waiting for transfers between devices: 15.5 us -> 0 us
  blocking collectives: 14.6 us -> 0 us
  other arithmetic: 13.7 us -> 24.5 us
  matrix products: 18.2 us -> 12.7 us
    pallas_call x0 -> x3, Pallas kernels: none -> 34.9 us  [the longest x2 30 us: with_halo(): pl.pallas_call(halo_kernel, out_shape=[jax.ShapeDtypeStruct(edge_rows.sha...]
    ppermute x8 -> x0, starting transfers between devices: 16.5 us -> none  [the longest x4 11.2 us: with_halo(): before = lax.ppermute(last, axis, up)]
    ppermute x8 -> x0, waiting for transfers between devices: 15.5 us -> none  [the longest x4 12 us: with_halo(): after = lax.ppermute(leading, axis, down)]
    psum x1 -> x0, blocking collectives: 14.6 us -> none  [local(): pooled = lax.psum(jnp.sum(act, axis=(2, 3)), ('row', 'col')) / pixels]
    another operation x0 -> x6, other arithmetic: none -> 8 us
    slice x2 -> x6, local copies, waits for them, and re-layouts: 0.05 us -> 6.95 us  [with_halo(): edge_rows = jnp.stack([own[:, 0, :], own[:, rows - 1, :]])]
    broadcast_in_dim x0 -> x5, other arithmetic: none -> 6.72 us  [the longest x2 6.64 us: with_halo(): return jnp.concatenate([left, mid, right], axis=2)[None]]
    convert_element_type x1 -> x0, other arithmetic: 4.74 us -> none  [local(): grad_pre = (grad_hidden * silu_slope(pre)).astype(jnp.bfloat16)]
  transfers between devices with their start and end apart: 8 -> 0, of which waited for: 5 -> 0; matrix products, arithmetic and copies ran while one was open for 2% -> 0% of each run, Pallas kernels for 0% -> 0%
where the time goes in v2:
time: 144 us; the launch traced here: 143 us
  Pallas kernels  72.2 us (50%)
  local copies, waits for them, and re-layouts  32.1 us (22%)
  other arithmetic  24.5 us (17%)
  matrix products  12.7 us (9%)
    pallas_call x1, Pallas kernels, sum_all(): pl.pallas_call(sum_kernel, out_shape=jax.ShapeDtypeStruct(laid.shape, f32...  37.3 us
    pallas_call x2, Pallas kernels, with_halo(): pl.pallas_call(halo_kernel, out_shape=[jax.ShapeDtypeStruct(edge_rows.sha...  30 us
    unnamed x51, local copies, waits for them, and re-layouts  8.8 us
    slice x6, local copies, waits for them, and re-layouts, with_halo(): edge_rows = jnp.stack([own[:, 0, :], own[:, rows - 1, :]])  6.95 us
    broadcast_in_dim x2, other arithmetic, with_halo(): return jnp.concatenate([left, mid, right], axis=2)[None]  6.64 us
    another operation x2, other arithmetic  6.06 us
    reduce_sum x1, other arithmetic, local(): jnp.sum(grad_conv.astype(jnp.float32) * hidden_pad[:, :, drow:drow + rows...  5.4 us
    pallas_call x1, Pallas kernels, sample_sum(): pl.pallas_call(sample_kernel, out_shape=jax.ShapeDtypeStruct(values.shape...  4.91 us

profile of v2, /device:TPU:0, one launch (start us, length us, event | category | flops | bytes accessed | tf_op | source)
XLA Modules:
  0.0 142.8 jit_solution(7223042511658764013)
XLA Ops:
  0.7 1.1 fusion.57
  1.8 1.7 %slice_reduce_fusion.8 = (f32[768]{0:T(1024)}, f32[768]{0:T(1024)}, f32[768]{0:T(1024)}, f32[768]{0:T(1024)}, f32[768]{0:T(1024)}, /*index=5*/f32[768]{0:T(1024)}, f32[768]{0:T(1024)}, f32[768]{0:T(1024)}, f32[768]{0:T(1024)}) fusion(f32[768,9]{0,1:T(8,128)} %param.11), kind=kLoop, calls=%fused_computation.155 | loop fusion | bytes 55296 | tf_op jit(solution)/shard_map/slice | solution.py:273
  3.5 1.1 fusion.58
  5.1 1.5 %copy.173 = bf16[192,8,128]{0,1,2:T(8,128)(2,1)S(1)} copy(bf16[192,8,128]{2,1,0:T(8,128)(2,1)} %bitcast.202) | data formatting | bytes 786432 | tf_op jit(solution)/shard_map/reshape.24
  6.6 3.5 %fusion.23 = (bf16[768,8,128]{0,1,2:T(8,128)(2,1)S(1)}, f32[8,128,768]{2,0,1:T(8,128)}) fusion(bf16[192,8,128]{0,1,2:T(8,128)(2,1)S(1)} %copy.162, bf16[192,768]{1,0:T(8,128)(2,1)} %param.10), kind=kOutput, calls=%fused_computation.49 | convolution fusion | flops 305922048 | bytes 5406720 | tf_op jit(solution)/shard_map/bchw,ce->behw/dot_general | solution.py:264
  10.2 1.3 fusion.98
  11.4 1.2 copy.147
  12.6 1.0 copy.148
  14.6 16.2 %halo.2 = (bf16[2,768,128]{2,1,0:T(8,128)(2,1)S(1)}, bf16[6,16,768]{2,1,0:T(8,128)(2,1)S(1)}) custom-call(bf16[2,768,128]{2,1,0:T(8,128)(2,1)S(1)} %pad_maximum_fusion.rows_ref, bf16[2,16,768]{2,1,0:T(8,128)(2,1)S(1)} %fusion.69.cols_ref), custom_call_target="tpu_custom_call" | custom-call | tf_op jit(solution)/shard_map/halo/pallas_call | solution.py:169
  31.6 1.3 copy.149
  32.9 1.0 copy.150
  34.0 3.3 %maximum_bitcast_fusion = bf16[1,768,10,130]{1,2,3,0:T(8,128)(2,1)S(1)} fusion(bf16[768,10,1]{0,1,2:T(8,128)(2,1)S(1)} %get-tuple-element.121, bf16[768,1,128]{0,1,2:T(2,128)(2,1)} %copy.150, bf16[768,8,128]{0,1,2:T(8,128)(2,1)S(1)} %get-tuple-element.114, bf16[768,1,128]{0,1,2:T(2,128)(2,1)S(1)} %copy.149, bf16[768,10,1]{0,1,2:T(8,128)(2,1)S(1)} %get-tuple-element.120), kind=kLoop, calls=%fused_computation.18 | loop fusion | flops 9984000 | bytes 3993600 | tf_op jit(solution)/shard_map/broadcast_in_dim | solution.py:196
  37.4 4.9 %fusion.91 = (f32[768]{0:T(1024)S(1)}, f32[768]{0:T(1024)S(1)}, f32[1,768,8,128]{1,2,3,0:T(8,128)S(1)}, f32[768,8,128]{0,1,2:T(8,128)S(1)}) fusion(bf16[1,768,10,130]{1,2,3,0:T(8,128)(2,1)S(1)} %maximum_bitcast_fusion, f32[768]{0:T(1024)S(1)} %copy-done.17, f32[768]{0:T(1024)S(1)} %copy-done.18, f32[768]{0:T(1024)S(1)} %copy-done.11, ...), kind=kOutput, calls=%fused_computation.165 | convolution fusion | flops 327940608 | bytes 21169152 | tf_op jit(solution)/shard_map/bchw,ec->behw/dot_general | solution.py:288
  42.3 4.9 %sample_sum.1 = f32[2,768]{1,0:T(2,128)S(1)} custom-call(f32[2,768]{1,0:T(2,128)S(1)} %pad_maximum_fusion.2.v_ref), custom_call_target="tpu_custom_call" | custom-call | tf_op jit(solution)/shard_map/sample_sum/pallas_call | solution.py:233
  48.3 5.4 %fusion.16 = (f32[768]{0:T(1024)S(1)}, f32[768]{0:T(1024)S(1)}, f32[768]{0:T(1024)S(1)}, f32[768]{0:T(1024)S(1)}, f32[768]{0:T(1024)S(1)}, /*index=5*/f32[768]{0...) fusion(bf16[1,768,10,130]{1,2,3,0:T(8,128)(2,1)S(1)} %maximum_b, ...), kind=kLoop, calls=%fused_computation.36 | loop fusion | flops 33023232 | bytes 23632896 | tf_op jit(solution)/shard_map/reduce_sum | solution.py:324
  56.7 1.3 convolution_bitcast_fusion.1
  58.7 1.0 copy.170
  61.2 1.3 fusion.97
  62.5 1.2 copy.155
  63.7 1.0 copy.156
  65.7 13.8 %halo.3 = (bf16[2,768,128]{2,1,0:T(8,128)(2,1)S(1)}, bf16[6,16,768]{2,1,0:T(8,128)(2,1)S(1)}) custom-call(bf16[2,768,128]{2,1,0:T(8,128)(2,1)S(1)} %pad_maximum_fusion.1.rows_ref, bf16[2,16,768]{2,1,0:T(8,128)(2,1)S(1)} %fusion.70.cols_ref), custom_call_target="tpu_custom_call" | custom-call | tf_op jit(solution)/shard_map/halo/pallas_call | solution.py:169
  80.3 1.3 copy.157
  81.6 1.0 copy.158
  82.7 3.4 %maximum_bitcast_fusion.1 = bf16[1,768,10,130]{1,2,3,0:T(8,128)(2,1)S(1)} fusion(bf16[768,10,1]{0,1,2:T(8,128)(2,1)S(1)} %fusion.74, bf16[768,1,128]{0,1,2:T(2,128)(2,1)} %copy.158, bf16[768,8,128]{0,1,2:T(8,128)(2,1)S(1)} %bitcast.201, bf16[768,1,128]{0,1,2:T(2,128)(2,1)S(1)} %copy.157, bf16[768,10,1]{0,1,2:T(8,128)(2,1)S(1)} %fusion.73), kind=kLoop, calls=%fused_computation.19 | loop fusion | flops 9984000 | bytes 3993600 | tf_op jit(solution)/shard_map/broadcast_in_dim | solution.py:196
  86.1 4.9 %fusion.32 = bf16[768,8,128]{0,1,2:T(8,128)(2,1)S(1)} fusion(f32[8,128,768]{2,0,1:T(8,128)S(1)} %copy-done.2, bf16[1,768,10,130]{1,2,3,0:T(8,128)(2,1)S(1)} %maximum_bitcast_fusion.1, f32[768]{0:T(1024)S(1)} %copy-done.17, f32[768]{0:T(1024)S(1)} %copy-done.18, f32[768]{0:T(1024)S(1)} %copy-done.11, f32[768]{0:T(1024)S(1)} %copy-done.12, ...), kind=kLoop, calls=%fused_computation.60 | loop fusion | flops 27525120 | bytes 18902016 | tf_op jit(solution)/shard_map/reshape.51
  93.4 1.0 copy.171
  94.4 3.0 %concatenate.39 = f32[768,490]{0,1:T(8,128)S(1)} concatenate(f32[768,192]{0,1:T(8,128)S(1)} %copy-done.3, f32[768,192]{0,1:T(8,128)S(1)} %convolution_bitcast_fusion, f32[768,1]{0,1:T(1,128)} %stack.59, f32[768,1]{0,1:T(1,128)S(1)} %stack.60, f32[768,1]{0,1:T(1,128)S(1)} %stack.61, f32[768,1]{0,1:T(1,128)S(1)} %stack.62, f32[768,1]{0,1:T(1,128)} %stack.63, f32[768,1]{0,1:T(1,128)} %stack.64, ...), dimensions={1} | concatenate | bytes 3010560 | tf_op jit(solution)/shard_map/concatenate | solution.py:353
  98.0 37.3 %sum_grads.1 = f32[2,4,4,24,512]{4,3,2,1,0:T(8,128)S(1)} custom-call(f32[2,4,4,24,512]{4,3,2,1,0:T(8,128)S(1)} %bitcast.198), custom_call_target="tpu_custom_call" | custom-call | tf_op jit(solution)/shard_map/sum_grads/pallas_call | solution.py:98
  136.8 1.0 fusion.96
  138.9 1.1 copy.181
  139.9 1.8 %copy.179 = f32[768,48]{0,1:T(8,128)} copy(f32[768,48]{1,0:T(8,128)} %get-tuple-element.86) | data formatting | bytes 294912
  141.7 1.1 copy.177
  (95 shorter events, 15.6 us)
Async XLA Ops:
  0.6 36.6 %copy-start = (bf16[768,192]{0,1:T(8,128)(2,1)S(1)}, bf16[768,192]{0,1:T(8,128)(2,1)}, u32[]{:S(2)}) copy-start(bf16[768,192]{0,1:T(8,128)(2,1)} %param.14) | copy-start | bytes 884740
  1.8 1.7 %copy-start.8 = (f32[8,128]{1,0:T(8,128)}, f32[8,128]{1,0:T(8,128)S(1)}, u32[]{:S(2)}) copy-start(f32[8,128]{1,0:T(8,128)S(1)} %add_rsqrt_fusion) | copy-start | bytes 12292
  33.9 3.4 %copy-start.10 = (f32[768]{0:T(1024)S(1)}, f32[768]{0:T(1024)}, u32[]{:S(2)}) copy-start(f32[768]{0:T(1024)} %get-tuple-element.69) | copy-start | bytes 9220
  33.9 3.4 %copy-start.11 = (f32[768]{0:T(1024)S(1)}, f32[768]{0:T(1024)}, u32[]{:S(2)}) copy-start(f32[768]{0:T(1024)} %get-tuple-element.70) | copy-start | bytes 9220
  33.9 3.4 %copy-start.12 = (f32[768]{0:T(1024)S(1)}, f32[768]{0:T(1024)}, u32[]{:S(2)}) copy-start(f32[768]{0:T(1024)} %get-tuple-element.71) | copy-start | bytes 9220
  33.9 3.4 %copy-start.13 = (f32[768]{0:T(1024)S(1)}, f32[768]{0:T(1024)}, u32[]{:S(2)}) copy-start(f32[768]{0:T(1024)} %get-tuple-element.72) | copy-start | bytes 9220
  33.9 3.4 %copy-start.14 = (f32[768]{0:T(1024)S(1)}, f32[768]{0:T(1024)}, u32[]{:S(2)}) copy-start(f32[768]{0:T(1024)} %get-tuple-element.73) | copy-start | bytes 9220
  34.0 3.4 %copy-start.15 = (f32[768]{0:T(1024)S(1)}, f32[768]{0:T(1024)}, u32[]{:S(2)}) copy-start(f32[768]{0:T(1024)} %get-tuple-element.74) | copy-start | bytes 9220
  34.0 3.4 %copy-start.16 = (f32[768]{0:T(1024)S(1)}, f32[768]{0:T(1024)}, u32[]{:S(2)}) copy-start(f32[768]{0:T(1024)} %get-tuple-element.75) | copy-start | bytes 9220
  34.0 3.4 %copy-start.17 = (f32[768]{0:T(1024)S(1)}, f32[768]{0:T(1024)}, u32[]{:S(2)}) copy-start(f32[768]{0:T(1024)} %get-tuple-element.76) | copy-start | bytes 9220
  34.0 3.4 %copy-start.18 = (f32[768]{0:T(1024)S(1)}, f32[768]{0:T(1024)}, u32[]{:S(2)}) copy-start(f32[768]{0:T(1024)} %get-tuple-element.77) | copy-start | bytes 9220
  37.4 9.9 %copy-start.6 = (f32[768,48]{0,1:T(8,128)S(1)}, f32[768,48]{0,1:T(8,128)}, u32[]{:S(2)}) copy-start(f32[768,48]{0,1:T(8,128)} %param.12) | copy-start | bytes 442372
  37.4 10.1 %copy-start.5 = (f32[48,768]{1,0:T(8,128)S(1)}, f32[48,768]{1,0:T(8,128)}, u32[]{:S(2)}) copy-start(f32[48,768]{1,0:T(8,128)} %param.13) | copy-start | bytes 442372
  48.2 9.8 %copy-start.1 = (bf16[1,192,8,128]{3,2,1,0:T(8,128)(2,1)S(1)}, bf16[1,192,8,128]{3,2,1,0:T(8,128)(2,1)}, u32[]{:S(2)}) copy-start(bf16[1,192,8,128]{3,2,1,0:T(8,128)(2,1)} %param.8) | copy-start | bytes 1179652
  82.7 3.4 %copy-start.2 = (f32[8,128,768]{2,0,1:T(8,128)S(1)}, f32[8,128,768]{2,0,1:T(8,128)}, u32[]{:S(2)}) copy-start(f32[8,128,768]{2,0,1:T(8,128)} %get-tuple-element.115) | copy-start | bytes 9437188
  86.1 5.5 %copy-start.9 = (f32[8,128]{1,0:T(8,128)S(1)}, f32[8,128]{1,0:T(8,128)}, u32[]{:S(2)}) copy-start(f32[8,128]{1,0:T(8,128)} %copy-done.8) | copy-start | bytes 12292
  86.1 5.5 %copy-start.19 = (f32[192]{0:T(256)S(1)}, f32[192]{0:T(256)}, u32[]{:S(2)}) copy-start(f32[192]{0:T(256)} %param.9) | copy-start | bytes 2308
  86.1 5.5 %copy-start.20 = (bf16[192,768]{1,0:T(8,128)(2,1)S(1)}, bf16[192,768]{1,0:T(8,128)(2,1)}, u32[]{:S(2)}) copy-start(bf16[192,768]{1,0:T(8,128)(2,1)} %param.10) | copy-start | bytes 884740
  91.0 2.1 %copy-start.4 = (bf16[1,192,8,128]{3,2,1,0:T(8,128)(2,1)S(1)}, bf16[1,192,8,128]{3,2,1,0:T(8,128)(2,1)}, u32[]{:S(2)}) copy-start(bf16[1,192,8,128]{3,2,1,0:T(8,128)(2,1)} %param.15) | copy-start | bytes 1179652
  91.6 2.8 %copy-start.3 = (f32[768,192]{0,1:T(8,128)S(1)}, f32[768,192]{0,1:T(8,128)}, u32[]{:S(2)}) copy-start(f32[768,192]{0,1:T(8,128)} %convolution_bitcast_fusion.1) | copy-start | bytes 1769476
  91.6 2.8 %copy-start.7 = (f32[768,48]{0,1:T(8,128)S(1)}, f32[768,48]{0,1:T(8,128)}, u32[]{:S(2)}) copy-start(f32[768,48]{0,1:T(8,128)} %multiply_multiply_fusion.1) | copy-start | bytes 442372

commit v3 on v2

--- a/solution.py
+++ b/solution.py
@@ -35,53 +35,84 @@
         pl.semaphore_signal(barrier, inc=1, device_id=other, device_id_type=MESH)
     pl.semaphore_wait(barrier, len(others))
 
-    def copy(src, dst, n, to):
-        return pltpu.make_async_remote_copy(
+    width = chunk_of(v_ref.shape[-1])
+    chunks = range(v_ref.shape[-1] // width)
+    sent = []
+
+    def go(src, dst, n, k, to):
+        copy = pltpu.make_async_remote_copy(
             src_ref=src,
             dst_ref=dst,
-            send_sem=send.at[n],
-            recv_sem=recv.at[n],
+            send_sem=send.at[n, k],
+            recv_sem=recv.at[n, k],
             device_id=to,
             device_id_type=MESH,
         )
-
-    def run(copies):
-        for one in copies:
-            one.start()
-        for one in copies:
-            one.wait()
-
-    run([copy(v_ref.at[1 - core], mate_buf, 0, mate())])
-    acc1[...] = v_ref[core] + mate_buf[...]
-    n = 0
-    moves = []
-    for s in range(1, groups):
-        at, to = peer(s)
-        moves.append(copy(acc1.at[at], group_buf.at[s - 1], n + s, to))
-    run(moves)
-    part = acc1[g]
-    for s in range(1, groups):
-        part = part + group_buf[s - 1]
-    acc2[...] = part
-    n += groups - 1
-    moves = []
-    for s in range(1, deep):
-        at, to = layer(s)
-        moves.append(copy(acc2.at[at], deep_buf.at[s - 1], n + s, to))
-    run(moves)
-    part = acc2[d]
-    for s in range(1, deep):
-        part = part + deep_buf[s - 1]
-    out_ref[core, g, d] = part
+        copy.start()
+        sent.append(copy)
+        return copy
+
+    cuts = [pl.ds(k * width, width) for k in chunks]
+    arriving = []
+    for k in chunks:
+        src = v_ref.at[1 - core, :, :, :, cuts[k]]
+        arriving.append([go(src, mate_buf.at[:, :, :, cuts[k]], 0, k, mate())])
+
+    def landed(k):
+        for copy in arriving[k]:
+            copy.wait_recv()
+        arriving[k] = []
+
+    for k in chunks:
+        landed(k)
+        cut = cuts[k]
+        acc1[:, :, :, cut] = v_ref[core, :, :, :, cut] + mate_buf[:, :, :, cut]
+        for s in range(1, groups):
+            at, to = peer(s)
+            src, dst = acc1.at[at, :, :, cut], group_buf.at[s - 1, :, :, cut]
+            arriving[k].append(go(src, dst, s, k, to))
+    n = groups - 1
+    for k in chunks:
+        landed(k)
+        cut = cuts[k]
+        part = acc1[g, :, :, cut]
+        for s in range(1, groups):
+            part = part + group_buf[s - 1, :, :, cut]
+        acc2[:, :, cut] = part
+        for s in range(1, deep):
+            at, to = layer(s)
+            src, dst = acc2.at[at, :, cut], deep_buf.at[s - 1, :, cut]
+            arriving[k].append(go(src, dst, n + s, k, to))
     n += deep - 1
-    mine = out_ref.at[core, g, d]
-    run([copy(mine, mine, n + s, layer(s)[1]) for s in range(1, deep)])
+    for k in chunks:
+        landed(k)
+        cut = cuts[k]
+        part = acc2[d, :, cut]
+        for s in range(1, deep):
+            part = part + deep_buf[s - 1, :, cut]
+        out_ref[core, g, d, :, cut] = part
+        mine = out_ref.at[core, g, d, :, cut]
+        for s in range(1, deep):
+            arriving[k].append(go(mine, mine, n + s, k, layer(s)[1]))
     n += deep - 1
-    mine = out_ref.at[core, g]
-    run([copy(mine, mine, n + s, peer(s)[1]) for s in range(1, groups)])
+    for k in chunks:
+        landed(k)
+        mine = out_ref.at[core, g, :, :, cuts[k]]
+        for s in range(1, groups):
+            arriving[k].append(go(mine, mine, n + s, k, peer(s)[1]))
     n += groups
-    mine = out_ref.at[core]
-    run([copy(mine, mine, n, mate())])
+    for k in chunks:
+        landed(k)
+        mine = out_ref.at[core, :, :, :, cuts[k]]
+        arriving[k].append(go(mine, mine, n, k, mate()))
+    for k in chunks:
+        landed(k)
+    for copy in sent:
+        copy.wait_send()
+
+
+def chunk_of(wide):
+    return 256 if wide % 256 == 0 else wide
 
 
 def sum_all(values):
@@ -106,8 +137,8 @@
             pltpu.VMEM((max(groups - 1, 1), deep, each, wide), f32),
             pltpu.VMEM((deep, each, wide), f32),
             pltpu.VMEM((max(deep - 1, 1), each, wide), f32),
-            pltpu.SemaphoreType.DMA((count,)),
-            pltpu.SemaphoreType.DMA((count,)),
+            pltpu.SemaphoreType.DMA((count, wide // chunk_of(wide))),
+            pltpu.SemaphoreType.DMA((count, wide // chunk_of(wide))),
         ],
         compiler_params=pltpu.CompilerParams(
             collective_id=0, has_side_effects=True, vmem_limit_bytes=48 << 20
@@ -131,40 +162,49 @@
     def at(drow, dcol):
         return (d, lax.rem(w + drow + count, count), lax.rem(c + dcol + wide, wide))
 
+    up, down, left, right = w > 0, w < count - 1, c > 0, c < wide - 1
+    rows_there = {-1: up, 0: True, 1: down}
+    cols_there = {-1: left, 0: True, 1: right}
     plan = [
-        (rows_ref.at[1], got_rows.at[0], at(1, 0)),
-        (rows_ref.at[0], got_rows.at[1], at(-1, 0)),
+        (rows_ref.at[1], got_rows.at[0], 1, 0),
+        (rows_ref.at[0], got_rows.at[1], -1, 0),
     ]
     for side, dcol in enumerate((1, -1)):
         for drow in (-1, 0, 1):
             slot = got_cols.at[side * 3 + 1 - drow]
-            plan.append((cols_ref.at[1 - side], slot, at(drow, dcol)))
-    greet([to for _, _, to in plan])
+            plan.append((cols_ref.at[1 - side], slot, drow, dcol))
+    greet([at(drow, dcol) for _, _, drow, dcol in plan])
+
+    def there(drow, dcol):
+        return jnp.logical_and(rows_there[drow], cols_there[dcol])
+
     copies = [
         pltpu.make_async_remote_copy(
             src_ref=src,
             dst_ref=dst,
             send_sem=send.at[n],
             recv_sem=recv.at[n],
-            device_id=to,
+            device_id=at(drow, dcol),
             device_id_type=MESH,
         )
-        for n, (src, dst, to) in enumerate(plan)
+        for n, (src, dst, drow, dcol) in enumerate(plan)
     ]
-    for copy in copies:
-        copy.start()
-    for copy in copies:
-        copy.wait()
+    for copy, (_, _, drow, dcol) in zip(copies, plan):
+        pl.when(there(drow, dcol))(copy.start)
+    for copy, (_, _, drow, dcol) in zip(copies, plan):
+        pl.when(there(-drow, -dcol))(copy.wait_recv)
+    for copy, (_, _, drow, dcol) in zip(copies, plan):
+        pl.when(there(drow, dcol))(copy.wait_send)
 
 
 def with_halo(shard, number):
     _, chans, rows, cols = shard.shape
     count, wide = lax.axis_size("row"), lax.axis_size("col")
     w, c = lax.axis_index("row"), lax.axis_index("col")
-    own = shard[0]
+    own = shard[0].transpose(1, 2, 0)
     tall = -(-rows // 16) * 16
-    edge_rows = jnp.stack([own[:, 0, :], own[:, rows - 1, :]])
-    edge_cols = jnp.stack([own[:, :, 0].T, own[:, :, cols - 1].T])
+    edge_rows = jnp.stack([own[0], own[rows - 1]])
+    edge_cols = jnp.stack([own[:, 0], own[:, cols - 1]])
     edge_cols = jnp.pad(edge_cols, ((0, 0), (0, tall - rows), (0, 0)))
     got_rows, got_cols = pl.pallas_call(
         halo_kernel,
@@ -182,18 +222,18 @@
     )(edge_rows, edge_cols)
     up, down = w > 0, w < count - 1
     zero = jnp.zeros((), shard.dtype)
-    above = jnp.where(up, got_rows[0], zero)[:, None, :]
-    below = jnp.where(down, got_rows[1], zero)[:, None, :]
+    above = jnp.where(up, got_rows[0], zero)[None]
+    below = jnp.where(down, got_rows[1], zero)[None]
 
     def side(got, there):
         top = jnp.where(up, got[0, rows - 1 : rows], zero)
         bottom = jnp.where(down, got[2, 0:1], zero)
         whole = jnp.concatenate([top, got[1, :rows], bottom], axis=0)
-        return jnp.where(there, whole, zero).T[:, :, None]
-
-    mid = jnp.concatenate([above, own, below], axis=1)
+        return jnp.where(there, whole, zero)[:, None]
+
+    mid = jnp.concatenate([above, own, below], axis=0)
     left, right = side(got_cols[:3], c > 0), side(got_cols[3:], c < wide - 1)
-    return jnp.concatenate([left, mid, right], axis=2)[None]
+    return jnp.concatenate([left, mid, right], axis=1).transpose(2, 0, 1)[None]
 
 
 def sample_kernel(v_ref, out_ref, buf, send, recv):
@@ -299,14 +339,14 @@
     gated = (act * excite[:, :, None, None]).astype(jnp.bfloat16)
     proj = jnp.einsum("behw,ec->bchw", gated, w_project, preferred_element_type=jnp.float32)
     output = (inputs.astype(jnp.float32) + proj).astype(jnp.bfloat16)
-    grad_project = jnp.einsum("behw,bchw->ec", gated, cotangent, preferred_element_type=jnp.float32)
+    grad_project = jnp.einsum("bchw,behw->ce", cotangent, gated, preferred_element_type=jnp.float32)
     grad_excite = sums[batch:]
     grad_epre = grad_excite * excite * (1.0 - excite)
     grad_wexc = jnp.einsum("bs,be->se", squeezed, grad_epre, precision=HIGH)
     grad_spre = jnp.einsum("be,se->bs", grad_epre, w_excite, precision=HIGH) * silu_slope(
         squeeze_pre
     )
-    grad_wsq = jnp.einsum("be,bs->es", pooled, grad_spre, precision=HIGH)
+    grad_wsq = jnp.einsum("bs,be->se", grad_spre, pooled, precision=HIGH)
     grad_pooled = jnp.einsum("bs,es->be", grad_spre, w_squeeze, precision=HIGH)
     grad_act = grad_gated * excite[:, :, None, None] + (grad_pooled / pixels)[:, :, None, None]
     grad_conv = (grad_act * silu_slope(conv)).astype(jnp.bfloat16)
@@ -327,7 +367,7 @@
                 axis=(0, 2, 3),
             )
         )
-    grad_kernel = jnp.stack(taps, axis=1)
+    grad_kernel = jnp.stack(taps, axis=0)
     grad_pre = (grad_hidden * silu_slope(pre)).astype(jnp.bfloat16)
     grad_wexp = jnp.einsum("bchw,behw->ce", scaled, grad_pre, preferred_element_type=jnp.float32)
     grad_scaled = jnp.einsum(
@@ -340,21 +380,21 @@
     ) + cotangent.astype(jnp.float32)
     lead = jnp.logical_and(lax.axis_index("row") == 0, lax.axis_index("col") == 0)
     keep = lead.astype(jnp.float32)
-    hidden_n = grad_project.shape[0]
+    hidden_n = grad_project.shape[1]
     pieces = [
         grad_project,
-        grad_wexp.T,
+        grad_wexp,
         grad_kernel,
         grad_wsq * keep,
-        grad_wexc.T * keep,
-        jnp.pad(grad_gain, (0, hidden_n - chans))[:, None],
+        grad_wexc * keep,
+        jnp.pad(grad_gain, (0, hidden_n - chans))[None],
     ]
-    sizes = [p.shape[1] for p in pieces]
-    total = sum_all(jnp.concatenate(pieces, axis=1))
+    sizes = [p.shape[0] for p in pieces]
+    total = sum_all(jnp.concatenate(pieces, axis=0))
     ends = [sum(sizes[: n + 1]) for n in range(len(sizes))]
-    parts = [total[:, e - n : e] for e, n in zip(ends, sizes)]
-    project_all, wexp_all, kernel_all = parts[0], parts[1].T, parts[2]
-    grad_wsq_all, grad_wexc_all, gain_all = parts[3], parts[4].T, parts[5][:chans, 0]
+    parts = [total[e - n : e] for e, n in zip(ends, sizes)]
+    project_all, wexp_all, kernel_all = parts[0].T, parts[1], parts[2].T
+    grad_wsq_all, grad_wexc_all, gain_all = parts[3].T, parts[4], parts[5][0, :chans]
     return (
         output,
         grad_in.astype(jnp.bfloat16),

time: 144 us -> 108 us (0.75)
  local copies, waits for them, and re-layouts: 32.1 us -> 12.4 us
  Pallas kernels: 72.2 us -> 56.7 us
  matrix products: 12.7 us -> 14.8 us
  other arithmetic: 24.5 us -> 22.9 us
    pallas_call x2, Pallas kernels: 30 us -> 19.6 us  [with_halo(): pl.pallas_call(halo_kernel, out_shape=[jax.ShapeDtypeStruct(edge_rows.sha...]
    unnamed x51 -> x26, local copies, waits for them, and re-layouts: 8.8 us -> 2.13 us
    slice x10 -> x4, local copies, waits for them, and re-layouts: 8.35 us -> 2.32 us  [the longest x2 1.02 us: with_halo(): edge_rows = jnp.stack([own[0], own[rows - 1]])]
    pallas_call x1, Pallas kernels: 37.3 us -> 32.2 us  [sum_all(): pl.pallas_call(sum_kernel, out_shape=jax.ShapeDtypeStruct(laid.shape, f32...]
    select_n x4 -> x0, local copies, waits for them, and re-layouts: 4.68 us -> none  [the longest x2 2.59 us: with_halo(): above = jnp.where(up, got_rows[0], zero)[:, None, :]]
    concatenate x1 -> x3, local copies, waits for them, and re-layouts: 2.98 us -> 0.77 us  [the longest x1 0.76 us: local(): total = sum_all(jnp.concatenate(pieces, axis=0))]
    broadcast_in_dim x5 -> x2, other arithmetic: 6.72 us -> 4.79 us  [with_halo(): return jnp.concatenate([left, mid, right], axis=1).transpose(2, 0, 1)[None]]
    transpose x0 -> x2, local copies, waits for them, and re-layouts: none -> 1.71 us  [local(): project_all, wexp_all, kernel_all = (parts[0].T, parts[1], parts[2].T)]
where the time goes in v3:
time: 108 us
  Pallas kernels  56.7 us (52%)
  other arithmetic  22.9 us (21%)
  matrix products  14.8 us (14%)
  local copies, waits for them, and re-layouts  12.4 us (11%)
  between operations  1.26 us (1%)
    pallas_call x1, Pallas kernels, sum_all(): pl.pallas_call(sum_kernel, out_shape=jax.ShapeDtypeStruct(laid.shape, f32...  32.2 us
    pallas_call x2, Pallas kernels, with_halo(): pl.pallas_call(halo_kernel, out_shape=[jax.ShapeDtypeStruct(edge_rows.sha...  19.6 us
    another operation x2, other arithmetic  6.06 us
    reduce_sum x1, other arithmetic, local(): jnp.sum(grad_conv.astype(jnp.float32) * hidden_pad[:, :, drow:drow + rows...  5.39 us
    pallas_call x1, Pallas kernels, sample_sum(): pl.pallas_call(sample_kernel, out_shape=jax.ShapeDtypeStruct(values.shape...  4.91 us
    dot_general x1, matrix products, local(): jnp.einsum('bchw,ec->behw', cotangent, w_project, preferred_element_type=...  4.9 us
    broadcast_in_dim x2, other arithmetic, with_halo(): return jnp.concatenate([left, mid, right], axis=1).transpose(2, 0, 1)[None]  4.79 us
    dot_general x1, matrix products, expand(): jnp.einsum('bchw,ce->behw', scaled, w_expand, preferred_element_type=jnp....  3.54 us

profile of v3, /device:TPU:0, one launch (start us, length us, event | category | flops | bytes accessed | tf_op | source)
XLA Modules:
  0.0 108.1 jit_solution(5486450531014385710)
XLA Ops:
  0.7 1.1 %fusion.51 = f32[8,128]{1,0:T(8,128)S(1)} fusion(bf16[1,192,8,128]{3,2,1,0:T(8,128)(2,1)} %param.8), kind=kLoop, calls=%fused_computation.82 | loop fusion | flops 588800 | bytes 397312 | tf_op jit(solution)/shard_map/reduce_sum | solution.py:297
  1.8 1.1 %slice_reduce_fusion.8 = (f32[768]{0:T(1024)S(1)}, f32[768]{0:T(1024)S(1)}, f32[768]{0:T(1024)S(1)}, f32[768]{0:T(1024)S(1)}, f32[768]{0:T(1024)S(1)}, /*index=5...) fusion(f32[768,9]{0,1:T(8,128)} %param.11), kind=kLoop, calls=%fused_computation.143 | loop fusion | bytes 55296 | tf_op jit(solution)/shard_map/slice | solution.py:313
  2.9 1.1 %fusion.52 = bf16[192,8,128]{2,0,1:T(8,128)(2,1)S(1)} fusion(f32[192]{0:T(256)} %param.9, f32[8,128]{1,0:T(8,128)S(1)} %add_rsqrt_fusion, bf16[1,192,8,128]{3,2,1,0:T(8,128)(2,1)} %param.8), kind=kLoop, calls=%fused_computation.88 | loop fusion | flops 786432 | bytes 791296 | tf_op jit(solution)/shard_map/reshape.5
  4.1 1.6 %copy.47 = bf16[192,8,128]{0,1,2:T(8,128)(2,1)S(1)} copy(bf16[192,8,128]{2,1,0:T(8,128)(2,1)} %bitcast.150) | data formatting | bytes 786432 | tf_op jit(solution)/shard_map/reshape.24
  6.1 3.5 %multiply_convert_fusion.1 = (bf16[8,128,768]{2,0,1:T(8,128)(2,1)S(1)}, f32[8,128,768]{2,0,1:T(8,128)}) fusion(bf16[192,8,128]{0,1,2:T(8,128)(2,1)S(1)} %copy.45, bf16[192,768]{1,0:T(8,128)(2,1)} %param.10), kind=kOutput, calls=%fused_computation.53 | convolution fusion | flops 305922048 | bytes 5406720 | tf_op jit(solution)/shard_map/bchw,ce->behw/dot_general | solution.py:304
  10.2 0.9 pad_maximum_fusion
  11.2 10.7 %halo.2 = (bf16[2,128,768]{2,1,0:T(8,128)(2,1)S(1)}, bf16[6,16,768]{2,1,0:T(8,128)(2,1)S(1)}) custom-call(bf16[2,128,768]{2,1,0:T(8,128)(2,1)S(1)} %copy.19.rows_ref, bf16[2,16,768]{2,1,0:T(8,128)(2,1)S(1)} %fusion.63.cols_ref), custom_call_target="tpu_custom_call" | custom-call | tf_op jit(solution)/shard_map/halo/pallas_call | solution.py:209
  22.4 0.9 broadcast_select_fusion.3
  23.3 2.5 %maximum_bitcast_fusion = bf16[1,768,10,130]{1,2,3,0:T(8,128)(2,1)S(1)} fusion(bf16[10,1,768]{2,0,1:T(8,128)(2,1)S(1)} %get-tuple-element.89, bf16[1,128,768]{2,0,1:T(2,128)(2,1)S(1)} %get-tuple-element.66, bf16[8,128,768]{2,0,1:T(8,128)(2,1)S(1)} %get-tuple-element.82, bf16[1,128,768]{2,0,1:T(2,128)(2,1)S(1)} %get-tuple-element.65, ...), kind=kLoop, calls=%fused_computation.18 | loop fusion | flops 9984000 | bytes 3993600 | tf_op jit(solution)/shard_map/broadcast_in_dim | solution.py:236
  25.8 4.9 %fusion.73 = (f32[768]{0:T(1024)S(1)}, f32[768]{0:T(1024)S(1)}, f32[1,768,8,128]{1,2,3,0:T(8,128)S(1)}, f32[768,8,128]{0,1,2:T(8,128)S(1)}) fusion(bf16[1,768,10,130]{1,2,3,0:T(8,128)(2,1)S(1)} %maximum_bitcast_fusion, f32[768]{0:T(1024)S(1)} %get-tuple-element.44, f32[768]{0:T(1024)S(1)} %get-tuple-element.45, f32[768]{0:T(1024)S(1)} %get-tuple-element.38, ...), kind=kOutput, calls=%fused_computation.153 | convolution fusion | flops 327940608 | bytes 21169152 | tf_op jit(solution)/shard_map/bchw,ec->behw/dot_general | solution.py:328
  30.8 4.9 %sample_sum.1 = f32[2,768]{1,0:T(2,128)S(1)} custom-call(f32[2,768]{1,0:T(2,128)S(1)} %pad_maximum_fusion.2.v_ref), custom_call_target="tpu_custom_call" | custom-call | tf_op jit(solution)/shard_map/sample_sum/pallas_call | solution.py:273
  36.7 5.4 %fusion.16 = (f32[768]{0:T(1024)S(1)}, f32[768]{0:T(1024)S(1)}, f32[768]{0:T(1024)S(1)}, f32[768]{0:T(1024)S(1)}, f32[768]{0:T(1024)S(1)}, /*index=5*/f32[768]{0...) fusion(bf16[1,768,10,130]{1,2,3,0:T(8,128)(2,1)S(1)} %maximum_b, ...), kind=kLoop, calls=%fused_computation.36 | loop fusion | flops 33023232 | bytes 23632896 | tf_op jit(solution)/shard_map/reduce_sum | solution.py:364
  42.2 1.3 %convolution_bitcast_fusion.2 = f32[192,768]{1,0:T(8,128)} fusion(bf16[768,8,128]{0,1,2:T(8,128)(2,1)S(1)} %get-tuple-element.50, bf16[192,8,128]{0,1,2:T(8,128)(2,1)S(1)} %copy.47), kind=kOutput, calls=%fused_computation.62 | convolution fusion | flops 301989888 | bytes 2555904 | tf_op jit(solution)/shard_map/bchw,behw->ce/dot_general | solution.py:342
  43.6 0.7 fusion.36
  44.3 1.0 copy.43
  45.3 0.7 multiply_multiply_fusion.1
  46.1 0.7 multiply_multiply_fusion
  47.3 0.9 pad_maximum_fusion.1
  48.3 8.9 %halo.3 = (bf16[2,128,768]{2,1,0:T(8,128)(2,1)S(1)}, bf16[6,16,768]{2,1,0:T(8,128)(2,1)S(1)}) custom-call(bf16[2,128,768]{2,1,0:T(8,128)(2,1)S(1)} %copy.30.rows_ref, bf16[2,16,768]{2,1,0:T(8,128)(2,1)S(1)} %fusion.64.cols_ref), custom_call_target="tpu_custom_call" | custom-call | tf_op jit(solution)/shard_map/halo/pallas_call | solution.py:209
  57.8 0.9 broadcast_select_fusion.2
  58.7 2.3 %maximum_bitcast_fusion.1 = bf16[1,768,10,130]{1,2,3,0:T(8,128)(2,1)S(1)} fusion(bf16[10,1,768]{2,0,1:T(8,128)(2,1)S(1)} %maximum_select_fusion.3, bf16[1,128,768]{2,0,1:T(2,128)(2,1)S(1)} %get-tuple-element.64, bf16[8,128,768]{2,0,1:T(8,128)(2,1)S(1)} %bitcast.149, bf16[1,128,768]{2,0,1:T(2,128)(2,1)S(1)} %get-tuple-element.63, ...), kind=kLoop, calls=%fused_computation.19 | loop fusion | flops 9984000 | bytes 3993600 | tf_op jit(solution)/shard_map/broadcast_in_dim | solution.py:236
  61.0 4.9 %fusion.29 = bf16[768,8,128]{0,1,2:T(8,128)(2,1)S(1)} fusion(f32[8,128,768]{2,0,1:T(8,128)S(1)} %copy-done.4, bf16[1,768,10,130]{1,2,3,0:T(8,128)(2,1)S(1)} %maximum_bitcast_fusion.1, f32[768]{0:T(1024)S(1)} %get-tuple-element.44, f32[768]{0:T(1024)S(1)} %get-tuple-element.45, f32[768]{0:T(1024)S(1)} %get-tuple-element.38, f32[768]{0:T(1024)S(1)} %get-tuple-element.39, ...), kind=kLoop, calls=%fused_computation.57 | loop fusion | flops 27525120 | bytes 18902016 | tf_op jit(solution)/shard_map/reshape.51
  66.0 1.2 %copy.38 = bf16[768,8,128]{2,0,1:T(8,128)(2,1)S(1)} copy(bf16[768,8,128]{0,1,2:T(8,128)(2,1)S(1)} %fusion.29) | data formatting | bytes 3145728 | tf_op jit(solution)/shard_map/reshape.51
  67.2 1.7 %convolution_bitcast_fusion.1 = f32[192,768]{1,0:T(8,128)S(1)} fusion(bf16[192,8,128]{2,0,1:T(8,128)(2,1)} %copy-done.1, bf16[768,8,128]{2,0,1:T(8,128)(2,1)S(1)} %copy.38), kind=kOutput, calls=%fused_computation.61 | convolution fusion | flops 301989888 | bytes 2555904 | tf_op jit(solution)/shard_map/bchw,behw->ce/dot_general | solution.py:372
  68.9 1.8 %fusion.50 = (f32[192]{0:T(256)S(1)}, f32[8,128]{1,0:T(8,128)S(1)}, f32[1,192,8,128]{3,1,2,0:T(8,128)S(1)}) fusion(f32[8,128]{1,0:T(8,128)S(1)} %add_rsqrt_fusion, bf16[1,192,8,128]{3,2,1,0:T(8,128)(2,1)} %param.8, f32[192]{0:T(256)S(1)} %copy-done.11, bf16[768,8,128]{2,0,1:T(8,128)(2,1)S(1)} %copy.38, bf16[192,768]{1,0:T(8,128)(2,1)} %param.10), kind=kOutput, calls=%fused_computation.81 | convolution fusion | flops 303364928 | bytes 3057152 | tf_op jit(solution)/shard_map/ce,behw->bchw/dot_general | solution.py:373
  71.0 1.0 copy.44
  72.0 0.8 concatenate.79
  72.9 32.2 %sum_grads.1 = f32[2,4,4,16,768]{4,3,2,1,0:T(8,128)S(1)} custom-call(f32[2,4,4,16,768]{4,3,2,1,0:T(8,128)S(1)} %bitcast.142), custom_call_target="tpu_custom_call" | custom-call | tf_op jit(solution)/shard_map/sum_grads/pallas_call | solution.py:129
  105.1 0.6 slice.317
  105.7 0.6 slice_bitcast_fusion.2
  106.3 0.7 fusion.77
  107.0 1.1 %slice_bitcast_fusion = (f32[768,192]{0,1:T(8,128)}, f32[192,768]{1,0:T(8,128)}) fusion(f32[512,768]{1,0:T(8,128)S(1)} %bitcast.146), kind=kLoop, calls=%fused_computation.87 | loop fusion | bytes 2359296 | tf_op jit(solution)/shard_map/transpose | solution.py:396
  (69 shorter events, 4.0 us)
Async XLA Ops:
  0.6 25.2 %copy-start = (bf16[768,192]{0,1:T(8,128)(2,1)S(1)}, bf16[768,192]{0,1:T(8,128)(2,1)}, u32[]{:S(2)}) copy-start(bf16[768,192]{0,1:T(8,128)(2,1)} %param.14) | copy-start | bytes 884740
  4.1 5.6 %copy-start.1 = (bf16[192,8,128]{2,0,1:T(8,128)(2,1)}, bf16[192,8,128]{2,0,1:T(8,128)(2,1)S(1)}, u32[]{:S(2)}) copy-start(bf16[192,8,128]{2,0,1:T(8,128)(2,1)S(1)} %fusion.52) | copy-start | bytes 1179652
  25.8 9.9 %copy-start.8 = (f32[768,48]{0,1:T(8,128)S(1)}, f32[768,48]{0,1:T(8,128)}, u32[]{:S(2)}) copy-start(f32[768,48]{0,1:T(8,128)} %param.12) | copy-start | bytes 442372
  25.8 10.1 %copy-start.7 = (f32[48,768]{1,0:T(8,128)S(1)}, f32[48,768]{1,0:T(8,128)}, u32[]{:S(2)}) copy-start(f32[48,768]{1,0:T(8,128)} %param.13) | copy-start | bytes 442372
  36.7 6.9 %copy-start.2 = (bf16[1,192,8,128]{3,2,1,0:T(8,128)(2,1)S(1)}, bf16[1,192,8,128]{3,2,1,0:T(8,128)(2,1)}, u32[]{:S(2)}) copy-start(bf16[1,192,8,128]{3,2,1,0:T(8,128)(2,1)} %param.8) | copy-start | bytes 1179652
  58.7 2.3 %copy-start.4 = (f32[8,128,768]{2,0,1:T(8,128)S(1)}, f32[8,128,768]{2,0,1:T(8,128)}, u32[]{:S(2)}) copy-start(f32[8,128,768]{2,0,1:T(8,128)} %get-tuple-element.83) | copy-start | bytes 9437188
  65.9 2.9 %copy-start.11 = (f32[192]{0:T(256)S(1)}, f32[192]{0:T(256)}, u32[]{:S(2)}) copy-start(f32[192]{0:T(256)} %param.9) | copy-start | bytes 2308
  67.1 3.6 %copy-start.3 = (bf16[1,192,8,128]{3,2,1,0:T(8,128)(2,1)S(1)}, bf16[1,192,8,128]{3,2,1,0:T(8,128)(2,1)}, u32[]{:S(2)}) copy-start(bf16[1,192,8,128]{3,2,1,0:T(8,128)(2,1)} %param.8) | copy-start | bytes 1179652
  67.1 3.6 %copy-start.6 = (bf16[1,192,8,128]{3,2,1,0:T(8,128)(2,1)S(1)}, bf16[1,192,8,128]{3,2,1,0:T(8,128)(2,1)}, u32[]{:S(2)}) copy-start(bf16[1,192,8,128]{3,2,1,0:T(8,128)(2,1)} %param.15) | copy-start | bytes 1179652
  68.9 3.1 %copy-start.5 = (f32[192,768]{1,0:T(8,128)S(1)}, f32[192,768]{1,0:T(8,128)}, u32[]{:S(2)}) copy-start(f32[192,768]{1,0:T(8,128)} %convolution_bitcast_fusion.2) | copy-start | bytes 1769476
  68.9 3.1 %copy-start.9 = (f32[48,768]{1,0:T(8,128)S(1)}, f32[48,768]{1,0:T(8,128)}, u32[]{:S(2)}) copy-start(f32[48,768]{1,0:T(8,128)} %multiply_multiply_fusion.1) | copy-start | bytes 442372
  68.9 3.1 %copy-start.10 = (f32[48,768]{1,0:T(8,128)S(1)}, f32[48,768]{1,0:T(8,128)}, u32[]{:S(2)}) copy-start(f32[48,768]{1,0:T(8,128)} %multiply_multiply_fusion) | copy-start | bytes 442372

commit v4 on v3

--- a/solution.py
+++ b/solution.py
@@ -35,8 +35,10 @@
         pl.semaphore_signal(barrier, inc=1, device_id=other, device_id_type=MESH)
     pl.semaphore_wait(barrier, len(others))
 
-    width = chunk_of(v_ref.shape[-1])
-    chunks = range(v_ref.shape[-1] // width)
+    each = v_ref.shape[3]
+    step = 8 * -(-each // 24)
+    starts = range(0, each, step)
+    chunks = range(len(starts))
     sent = []
 
     def go(src, dst, n, k, to):
@@ -52,11 +54,11 @@
         sent.append(copy)
         return copy
 
-    cuts = [pl.ds(k * width, width) for k in chunks]
+    cuts = [pl.ds(at, min(step, each - at)) for at in starts]
     arriving = []
     for k in chunks:
-        src = v_ref.at[1 - core, :, :, :, cuts[k]]
-        arriving.append([go(src, mate_buf.at[:, :, :, cuts[k]], 0, k, mate())])
+        src = v_ref.at[1 - core, :, :, cuts[k]]
+        arriving.append([go(src, mate_buf.at[:, :, cuts[k]], 0, k, mate())])
 
     def landed(k):
         for copy in arriving[k]:
@@ -66,44 +68,44 @@
     for k in chunks:
         landed(k)
         cut = cuts[k]
-        acc1[:, :, :, cut] = v_ref[core, :, :, :, cut] + mate_buf[:, :, :, cut]
+        acc1[:, :, cut] = v_ref[core, :, :, cut] + mate_buf[:, :, cut]
         for s in range(1, groups):
             at, to = peer(s)
-            src, dst = acc1.at[at, :, :, cut], group_buf.at[s - 1, :, :, cut]
+            src, dst = acc1.at[at, :, cut], group_buf.at[s - 1, :, cut]
             arriving[k].append(go(src, dst, s, k, to))
     n = groups - 1
     for k in chunks:
         landed(k)
         cut = cuts[k]
-        part = acc1[g, :, :, cut]
+        part = acc1[g, :, cut]
         for s in range(1, groups):
-            part = part + group_buf[s - 1, :, :, cut]
-        acc2[:, :, cut] = part
+            part = part + group_buf[s - 1, :, cut]
+        acc2[:, cut] = part
         for s in range(1, deep):
             at, to = layer(s)
-            src, dst = acc2.at[at, :, cut], deep_buf.at[s - 1, :, cut]
+            src, dst = acc2.at[at, cut], deep_buf.at[s - 1, cut]
             arriving[k].append(go(src, dst, n + s, k, to))
     n += deep - 1
     for k in chunks:
         landed(k)
         cut = cuts[k]
-        part = acc2[d, :, cut]
+        part = acc2[d, cut]
         for s in range(1, deep):
-            part = part + deep_buf[s - 1, :, cut]
-        out_ref[core, g, d, :, cut] = part
-        mine = out_ref.at[core, g, d, :, cut]
+            part = part + deep_buf[s - 1, cut]
+        out_ref[core, g, d, cut] = part
+        mine = out_ref.at[core, g, d, cut]
         for s in range(1, deep):
             arriving[k].append(go(mine, mine, n + s, k, layer(s)[1]))
     n += deep - 1
     for k in chunks:
         landed(k)
-        mine = out_ref.at[core, g, :, :, cuts[k]]
+        mine = out_ref.at[core, g, :, cuts[k]]
         for s in range(1, groups):
             arriving[k].append(go(mine, mine, n + s, k, peer(s)[1]))
     n += groups
     for k in chunks:
         landed(k)
-        mine = out_ref.at[core, :, :, :, cuts[k]]
+        mine = out_ref.at[core, :, :, cuts[k]]
         arriving[k].append(go(mine, mine, n, k, mate()))
     for k in chunks:
         landed(k)
@@ -119,8 +121,9 @@
     rows, cols = values.shape
     groups = lax.axis_size("row") * (lax.axis_size("col") // 2)
     deep = lax.axis_size("dp")
-    each = -(-rows // (2 * groups * deep))
+    each = 8 * -(-rows // (16 * groups * deep))
     wide = -(-cols // 128) * 128
+    chunks = -(-each // (8 * -(-each // 24)))
     full = 2 * groups * deep * each
     laid = jnp.pad(values, ((0, full - rows), (0, wide - cols)))
     laid = laid.reshape(2, groups, deep, each, wide)
@@ -137,8 +140,8 @@
             pltpu.VMEM((max(groups - 1, 1), deep, each, wide), f32),
             pltpu.VMEM((deep, each, wide), f32),
             pltpu.VMEM((max(deep - 1, 1), each, wide), f32),
-            pltpu.SemaphoreType.DMA((count, wide // chunk_of(wide))),
-            pltpu.SemaphoreType.DMA((count, wide // chunk_of(wide))),
+            pltpu.SemaphoreType.DMA((count, chunks)),
+            pltpu.SemaphoreType.DMA((count, chunks)),
         ],
         compiler_params=pltpu.CompilerParams(
             collective_id=0, has_side_effects=True, vmem_limit_bytes=48 << 20
@@ -155,7 +158,10 @@
     pl.semaphore_wait(barrier, len(others))
 
 
-def halo_kernel(rows_ref, cols_ref, got_rows, got_cols, send, recv):
+def halo_kernel(*refs):
+    rows_ref, cols_ref = refs[:2]
+    got_rows, got_cols = refs[2:4] if len(refs) == 6 else refs[3:5]
+    send, recv = refs[-2:]
     d, w, c = (lax.axis_index(a) for a in ("dp", "row", "col"))
     count, wide = lax.axis_size("row"), lax.axis_size("col")
 
@@ -173,7 +179,11 @@
         for drow in (-1, 0, 1):
             slot = got_cols.at[side * 3 + 1 - drow]
             plan.append((cols_ref.at[1 - side], slot, drow, dcol))
-    greet([at(drow, dcol) for _, _, drow, dcol in plan])
+    layers = []
+    if len(refs) > 6:
+        deep = lax.axis_size("dp")
+        layers = [(lax.rem(d + s, deep), w, c) for s in range(1, deep)]
+    greet([at(drow, dcol) for _, _, drow, dcol in plan] + layers)
 
     def there(drow, dcol):
         return jnp.logical_and(rows_there[drow], cols_there[dcol])
@@ -189,15 +199,32 @@
         )
         for n, (src, dst, drow, dcol) in enumerate(plan)
     ]
+    extra = []
+    for n, to in enumerate(layers):
+        copy = pltpu.make_async_remote_copy(
+            src_ref=refs[2],
+            dst_ref=refs[5].at[d],
+            send_sem=send.at[len(plan) + n],
+            recv_sem=recv.at[len(plan) + n],
+            device_id=to,
+            device_id_type=MESH,
+        )
+        extra.append(copy)
     for copy, (_, _, drow, dcol) in zip(copies, plan):
         pl.when(there(drow, dcol))(copy.start)
+    for copy in extra:
+        copy.start()
+    if layers:
+        refs[5][d] = refs[2][...]
+    for copy in extra:
+        copy.wait()
     for copy, (_, _, drow, dcol) in zip(copies, plan):
         pl.when(there(-drow, -dcol))(copy.wait_recv)
     for copy, (_, _, drow, dcol) in zip(copies, plan):
         pl.when(there(drow, dcol))(copy.wait_send)
 
 
-def with_halo(shard, number):
+def with_halo(shard, number, vectors=None):
     _, chans, rows, cols = shard.shape
     count, wide = lax.axis_size("row"), lax.axis_size("col")
     w, c = lax.axis_index("row"), lax.axis_index("col")
@@ -206,20 +233,31 @@
     edge_rows = jnp.stack([own[0], own[rows - 1]])
     edge_cols = jnp.stack([own[:, 0], own[:, cols - 1]])
     edge_cols = jnp.pad(edge_cols, ((0, 0), (0, tall - rows), (0, 0)))
-    got_rows, got_cols = pl.pallas_call(
+    ins = [edge_rows, edge_cols]
+    outs = [
+        jax.ShapeDtypeStruct(edge_rows.shape, shard.dtype),
+        jax.ShapeDtypeStruct((6, tall, chans), shard.dtype),
+    ]
+    copies = 8
+    if vectors is not None:
+        deep = lax.axis_size("dp")
+        ins.append(vectors)
+        outs.append(jax.ShapeDtypeStruct((deep, *vectors.shape), vectors.dtype))
+        copies += deep - 1
+    got_rows, got_cols, *every = pl.pallas_call(
         halo_kernel,
-        out_shape=[
-            jax.ShapeDtypeStruct(edge_rows.shape, shard.dtype),
-            jax.ShapeDtypeStruct((6, tall, chans), shard.dtype),
+        out_shape=outs,
+        in_specs=[pl.BlockSpec(memory_space=pltpu.VMEM)] * len(ins),
+        out_specs=[pl.BlockSpec(memory_space=pltpu.VMEM)] * len(outs),
+        scratch_shapes=[
+            pltpu.SemaphoreType.DMA((copies,)),
+            pltpu.SemaphoreType.DMA((copies,)),
         ],
-        in_specs=[pl.BlockSpec(memory_space=pltpu.VMEM)] * 2,
-        out_specs=[pl.BlockSpec(memory_space=pltpu.VMEM)] * 2,
-        scratch_shapes=[pltpu.SemaphoreType.DMA((8,)), pltpu.SemaphoreType.DMA((8,))],
         compiler_params=pltpu.CompilerParams(
             collective_id=number, has_side_effects=True, vmem_limit_bytes=48 << 20
         ),
         name="halo",
-    )(edge_rows, edge_cols)
+    )(*ins)
     up, down = w > 0, w < count - 1
     zero = jnp.zeros((), shard.dtype)
     above = jnp.where(up, got_rows[0], zero)[None]
@@ -233,7 +271,8 @@
 
     mid = jnp.concatenate([above, own, below], axis=0)
     left, right = side(got_cols[:3], c > 0), side(got_cols[3:], c < wide - 1)
-    return jnp.concatenate([left, mid, right], axis=1).transpose(2, 0, 1)[None]
+    whole = jnp.concatenate([left, mid, right], axis=1).transpose(2, 0, 1)[None]
+    return (whole, *every) if every else whole
 
 
 def sample_kernel(v_ref, out_ref, buf, send, recv):
@@ -342,15 +381,20 @@
     grad_project = jnp.einsum("bchw,behw->ce", cotangent, gated, preferred_element_type=jnp.float32)
     grad_excite = sums[batch:]
     grad_epre = grad_excite * excite * (1.0 - excite)
-    grad_wexc = jnp.einsum("bs,be->se", squeezed, grad_epre, precision=HIGH)
     grad_spre = jnp.einsum("be,se->bs", grad_epre, w_excite, precision=HIGH) * silu_slope(
         squeeze_pre
     )
-    grad_wsq = jnp.einsum("bs,be->se", grad_spre, pooled, precision=HIGH)
     grad_pooled = jnp.einsum("bs,es->be", grad_spre, w_squeeze, precision=HIGH)
     grad_act = grad_gated * excite[:, :, None, None] + (grad_pooled / pixels)[:, :, None, None]
     grad_conv = (grad_act * silu_slope(conv)).astype(jnp.bfloat16)
-    grad_pad = with_halo(grad_conv, 2)
+    spare = ((0, 0), (0, pooled.shape[1] - squeezed.shape[1]))
+    vectors = [pooled, grad_epre, jnp.pad(squeezed, spare), jnp.pad(grad_spre, spare)]
+    grad_pad, every = with_halo(grad_conv, 2, jnp.concatenate(vectors))
+    every = every.reshape(-1, 4, *pooled.shape)
+    all_pooled, all_epre = every[:, 0], every[:, 1]
+    all_squeezed, all_spre = (every[:, n, :, : squeezed.shape[1]] for n in (2, 3))
+    grad_wsq_all = jnp.einsum("dbs,dbe->se", all_spre, all_pooled, precision=HIGH).T
+    grad_wexc_all = jnp.einsum("dbs,dbe->se", all_squeezed, all_epre, precision=HIGH)
     grad_hidden = jnp.zeros(pre.shape, jnp.float32)
     taps = []
     for tap in range(9):
@@ -378,23 +422,26 @@
     grad_in = inverse * (
         grad_normed - normed * jnp.mean(grad_normed * normed, axis=1, keepdims=True)
     ) + cotangent.astype(jnp.float32)
-    lead = jnp.logical_and(lax.axis_index("row") == 0, lax.axis_index("col") == 0)
-    keep = lead.astype(jnp.float32)
     hidden_n = grad_project.shape[1]
     pieces = [
         grad_project,
         grad_wexp,
         grad_kernel,
-        grad_wsq * keep,
-        grad_wexc * keep,
         jnp.pad(grad_gain, (0, hidden_n - chans))[None],
     ]
     sizes = [p.shape[0] for p in pieces]
-    total = sum_all(jnp.concatenate(pieces, axis=0))
+    height, width = sum(sizes), chunk_of(hidden_n)
+    starts = range(0, hidden_n, width)
+    total = sum_all(jnp.concatenate([p[:, k : k + width] for k in starts for p in pieces], axis=0))
     ends = [sum(sizes[: n + 1]) for n in range(len(sizes))]
-    parts = [total[e - n : e] for e, n in zip(ends, sizes)]
+    parts = [
+        jnp.concatenate(
+            [total[k * height + e - n : k * height + e] for k in range(len(starts))], axis=1
+        )
+        for e, n in zip(ends, sizes)
+    ]
     project_all, wexp_all, kernel_all = parts[0].T, parts[1], parts[2].T
-    grad_wsq_all, grad_wexc_all, gain_all = parts[3].T, parts[4], parts[5][0, :chans]
+    gain_all = parts[3][0, :chans]
     return (
         output,
         grad_in.astype(jnp.bfloat16),

time: 108 us -> 113 us (1.046)
  Pallas kernels: 56.7 us -> 53.4 us
  local copies, waits for them, and re-layouts: 12.4 us -> 15.7 us
  matrix products: 14.8 us -> 18 us
    pallas_call x1, Pallas kernels: 32.2 us -> 27.1 us  [sum_all(): pl.pallas_call(sum_kernel, out_shape=jax.ShapeDtypeStruct(laid.shape, f32...]
    concatenate x1, local copies, waits for them, and re-layouts: 0.76 us -> 4.75 us  [local(): jnp.concatenate([p[:, k:k + width] for k in starts for p in pieces], axis=0)]
    dot_general x0 -> x2, matrix products: none -> 1.99 us  [the longest x1 1 us: local(): jnp.einsum('dbs,dbe->se', all_squeezed, all_epre, precision=HIGH)]
    pallas_call x2, Pallas kernels: 19.6 us -> 21.3 us  [with_halo(): pl.pallas_call(halo_kernel, out_shape=outs, in_specs=[pl.BlockSpec(memory...]
    transpose x2 -> x0, local copies, waits for them, and re-layouts: 1.71 us -> none  [local(): project_all, wexp_all, kernel_all = (parts[0].T, parts[1], parts[2].T)]
    transpose x0 -> x2, other arithmetic: none -> 1.48 us  [local(): project_all, wexp_all, kernel_all = (parts[0].T, parts[1], parts[2].T)]
    mul x3 -> x1, other arithmetic: 1.51 us -> 0.05 us  [local(): squeezed = jax.nn.silu(squeeze_pre)]
    slice x2 -> x9, local copies, waits for them, and re-layouts: 1.3 us -> 2.28 us  [the longest x4 1.57 us: local(): p[:, k:k + width]]
where the time goes in v4:
time: 113 us; the launch traced here: 112 us
  Pallas kernels  53.4 us (47%)
  other arithmetic  23.8 us (21%)
  matrix products  18 us (16%)
  local copies, waits for them, and re-layouts  15.7 us (14%)
  between operations  1.54 us (1%)
    pallas_call x1, Pallas kernels, sum_all(): pl.pallas_call(sum_kernel, out_shape=jax.ShapeDtypeStruct(laid.shape, f32...  27.1 us
    pallas_call x2, Pallas kernels, with_halo(): pl.pallas_call(halo_kernel, out_shape=outs, in_specs=[pl.BlockSpec(memory...  21.3 us
    another operation x2, other arithmetic  6.06 us
    reduce_sum x1, other arithmetic, local(): jnp.sum(grad_conv.astype(jnp.float32) * hidden_pad[:, :, drow:drow + rows...  5.4 us
    pallas_call x1, Pallas kernels, sample_sum(): pl.pallas_call(sample_kernel, out_shape=jax.ShapeDtypeStruct(values.shape...  4.91 us
    dot_general x1, matrix products, local(): jnp.einsum('bchw,ec->behw', cotangent, w_project, preferred_element_type=...  4.9 us
    broadcast_in_dim x2, other arithmetic, with_halo(): whole = jnp.concatenate([left, mid, right], axis=1).transpose(2, 0, 1)[None]  4.79 us
    concatenate x1, local copies, waits for them, and re-layouts, local(): jnp.concatenate([p[:, k:k + width] for k in starts for p in pieces], axis=0)  4.75 us

profile of v4, /device:TPU:0, one launch (start us, length us, event | category | flops | bytes accessed | tf_op | source)
XLA Modules:
  0.0 112.4 jit_solution(18405700475483441976)
XLA Ops:
  0.7 1.1 fusion.51
  1.8 1.1 slice_reduce_fusion.8
  3.0 1.1 %fusion.52 = bf16[192,8,128]{2,0,1:T(8,128)(2,1)S(1)} fusion(f32[192]{0:T(256)} %param.9, f32[8,128]{1,0:T(8,128)S(1)} %add_rsqrt_fusion, bf16[1,192,8,128]{3,2,1,0:T(8,128)(2,1)} %param.8), kind=kLoop, calls=%fused_computation.89 | loop fusion | flops 786432 | bytes 791296 | tf_op jit(solution)/shard_map/reshape.6
  4.2 1.6 %copy.47 = bf16[192,8,128]{0,1,2:T(8,128)(2,1)S(1)} copy(bf16[192,8,128]{2,1,0:T(8,128)(2,1)} %bitcast.161) | data formatting | bytes 786432 | tf_op jit(solution)/shard_map/reshape.25
  6.2 3.5 %multiply_convert_fusion.1 = (bf16[8,128,768]{2,0,1:T(8,128)(2,1)S(1)}, f32[8,128,768]{2,0,1:T(8,128)}) fusion(bf16[192,8,128]{0,1,2:T(8,128)(2,1)S(1)} %copy.45, bf16[192,768]{1,0:T(8,128)(2,1)} %param.10), kind=kOutput, calls=%fused_computation.53 | convolution fusion | flops 305922048 | bytes 5406720 | tf_op jit(solution)/shard_map/bchw,ce->behw/dot_general | solution.py:343
  10.3 0.9 pad_maximum_fusion.1
  11.3 10.7 %halo.2 = (bf16[2,128,768]{2,1,0:T(8,128)(2,1)S(1)}, bf16[6,16,768]{2,1,0:T(8,128)(2,1)S(1)}) custom-call(bf16[2,128,768]{2,1,0:T(8,128)(2,1)S(1)} %copy.19.refs_0_, bf16[2,16,768]{2,1,0:T(8,128)(2,1)S(1)} %fusion.63.refs_1_), custom_call_target="tpu_custom_call" | custom-call | tf_op jit(solution)/shard_map/halo/pallas_call | solution.py:247
  22.5 0.9 broadcast_select_fusion.3
  23.4 2.5 %maximum_bitcast_fusion = bf16[1,768,10,130]{1,2,3,0:T(8,128)(2,1)S(1)} fusion(bf16[10,1,768]{2,0,1:T(8,128)(2,1)S(1)} %get-tuple-element.109, bf16[1,128,768]{2,0,1:T(2,128)(2,1)S(1)} %get-tuple-element.77, bf16[8,128,768]{2,0,1:T(8,128)(2,1)S(1)} %get-tuple-element.104, bf16[1,128,768]{2,0,1:T(2,128)(2,1)S(1)} %get-tuple-element.76, ...), kind=kLoop, calls=%fused_computation.18 | loop fusion | flops 9984000 | bytes 3993600 | tf_op jit(solution)/shard_map/broadcast_in_dim | solution.py:274
  26.0 4.9 %fusion.77 = (f32[768]{0:T(1024)S(1)}, f32[768]{0:T(1024)S(1)}, f32[1,768,8,128]{1,2,3,0:T(8,128)S(1)}, f32[768,8,128]{0,1,2:T(8,128)S(1)}) fusion(bf16[1,768,10,130]{1,2,3,0:T(8,128)(2,1)S(1)} %maximum_bitcast_fusion, f32[768]{0:T(1024)S(1)} %get-tuple-element.46, f32[768]{0:T(1024)S(1)} %get-tuple-element.47, f32[768]{0:T(1024)S(1)} %get-tuple-element.40, ...), kind=kOutput, calls=%fused_computation.162 | convolution fusion | flops 327940608 | bytes 21169152 | tf_op jit(solution)/shard_map/bchw,ec->behw/dot_general | solution.py:367
  31.0 4.9 %sample_sum.1 = f32[2,768]{1,0:T(2,128)S(1)} custom-call(f32[2,768]{1,0:T(2,128)S(1)} %pad_maximum_fusion.3.v_ref), custom_call_target="tpu_custom_call" | custom-call | tf_op jit(solution)/shard_map/sample_sum/pallas_call | solution.py:312
  36.9 5.4 %fusion.16 = (f32[768]{0:T(1024)S(1)}, f32[768]{0:T(1024)S(1)}, f32[768]{0:T(1024)S(1)}, f32[768]{0:T(1024)S(1)}, f32[768]{0:T(1024)S(1)}, /*index=5*/f32[768]{0...) fusion(bf16[1,768,10,130]{1,2,3,0:T(8,128)(2,1)S(1)} %maximum_b, ...), kind=kLoop, calls=%fused_computation.36 | loop fusion | flops 33023232 | bytes 23632896 | tf_op jit(solution)/shard_map/reduce_sum | solution.py:408
  42.5 1.6 %convolution_bitcast_fusion.2 = f32[192,768]{1,0:T(8,128)S(1)} fusion(bf16[768,8,128]{0,1,2:T(8,128)(2,1)S(1)} %get-tuple-element.50, bf16[192,8,128]{0,1,2:T(8,128)(2,1)} %copy-done.4), kind=kOutput, calls=%fused_computation.62 | convolution fusion | flops 301989888 | bytes 2555904 | tf_op jit(solution)/shard_map/bchw,behw->ce/dot_general | solution.py:381
  44.1 1.7 %fusion.36 = bf16[1,192,8,128]{3,1,2,0:T(8,128)(2,1)S(1)} fusion(bf16[768,8,128]{0,1,2:T(8,128)(2,1)S(1)} %get-tuple-element.50, bf16[768,192]{0,1:T(8,128)(2,1)S(1)} %copy-done, bf16[1,192,8,128]{3,2,1,0:T(8,128)(2,1)} %param.8), kind=kOutput, calls=%fused_computation.63 | convolution fusion | flops 302579712 | bytes 2654208 | tf_op jit(solution)/shard_map/behw,ec->bchw/dot_general | solution.py:379
  45.8 1.0 copy.43
  46.8 0.8 fusion.85
  48.2 0.9 pad_maximum_fusion.2
  49.1 10.7 %halo.3 = (bf16[2,128,768]{2,1,0:T(8,128)(2,1)S(1)}, bf16[6,16,768]{2,1,0:T(8,128)(2,1)S(1)}, f32[4,4,768]{2,1,0:T(4,128)S(1)}) custom-call(bf16[2,128,768]{2,1,0:T(8,128)(2,1)S(1)} %copy.30.refs_0_, bf16[2,16,768]{2,1,0:T(8,128)(2,1)S(1)} %fusion.64.refs_1_, f32[4,768]{1,0:T(4,128)S(1)} %select_maximum_fusion.refs_2_), custom_call_target="tpu_custom_call" | custom-call | tf_op jit(solution)/shard_map/halo/pallas_call | solution.py:247
  60.4 1.0 fusion.68
  61.4 1.0 fusion.65
  62.4 0.9 broadcast_select_fusion.2
  63.4 2.3 %maximum_bitcast_fusion.1 = bf16[1,768,10,130]{1,2,3,0:T(8,128)(2,1)S(1)} fusion(bf16[10,1,768]{2,0,1:T(8,128)(2,1)S(1)} %maximum_select_fusion.3, bf16[1,128,768]{2,0,1:T(2,128)(2,1)S(1)} %get-tuple-element.75, bf16[8,128,768]{2,0,1:T(8,128)(2,1)S(1)} %bitcast.160, bf16[1,128,768]{2,0,1:T(2,128)(2,1)S(1)} %get-tuple-element.74, ...), kind=kLoop, calls=%fused_computation.19 | loop fusion | flops 9984000 | bytes 3993600 | tf_op jit(solution)/shard_map/broadcast_in_dim | solution.py:274
  65.8 4.9 %fusion.29 = bf16[768,8,128]{0,1,2:T(8,128)(2,1)S(1)} fusion(f32[8,128,768]{2,0,1:T(8,128)S(1)} %copy-done.3, bf16[1,768,10,130]{1,2,3,0:T(8,128)(2,1)S(1)} %maximum_bitcast_fusion.1, f32[768]{0:T(1024)S(1)} %copy-done.23, f32[768]{0:T(1024)S(1)} %copy-done.25, f32[768]{0:T(1024)S(1)} %copy-done.11, f32[768]{0:T(1024)S(1)} %copy-done.13, ...), kind=kLoop, calls=%fused_computation.57 | loop fusion | flops 27525120 | bytes 18902016 | tf_op jit(solution)/shard_map/reshape.52
  70.8 1.2 %copy.38 = bf16[768,8,128]{2,0,1:T(8,128)(2,1)S(1)} copy(bf16[768,8,128]{0,1,2:T(8,128)(2,1)S(1)} %fusion.29) | data formatting | bytes 3145728 | tf_op jit(solution)/shard_map/reshape.52
  72.0 1.7 %convolution_bitcast_fusion.1 = f32[192,768]{1,0:T(8,128)S(1)} fusion(bf16[192,8,128]{2,0,1:T(8,128)(2,1)} %copy-done.1, bf16[768,8,128]{2,0,1:T(8,128)(2,1)S(1)} %copy.38), kind=kOutput, calls=%fused_computation.61 | convolution fusion | flops 301989888 | bytes 2555904 | tf_op jit(solution)/shard_map/bchw,behw->ce/dot_general | solution.py:416
  73.7 1.8 %fusion.50 = (f32[192]{0:T(256)S(1)}, f32[8,128]{1,0:T(8,128)S(1)}, f32[1,192,8,128]{3,1,2,0:T(8,128)S(1)}) fusion(f32[8,128]{1,0:T(8,128)S(1)} %add_rsqrt_fusion, bf16[1,192,8,128]{3,2,1,0:T(8,128)(2,1)} %param.8, f32[192]{0:T(256)S(1)} %copy-done.26, bf16[768,8,128]{2,0,1:T(8,128)(2,1)S(1)} %copy.38, bf16[192,768]{1,0:T(8,128)(2,1)} %param.10), kind=kOutput, calls=%fused_computation.81 | convolution fusion | flops 303364928 | bytes 3057152 | tf_op jit(solution)/shard_map/ce,behw->bchw/dot_general | solution.py:417
  75.4 0.7 fusion.84
  76.2 4.7 %concatenate.92 = f32[1182,256]{1,0:T(8,128)S(1)} concatenate(f32[192,256]{1,0:T(8,128)} %get-tuple-element.73, f32[192,256]{1,0:T(8,128)} %get-tuple-element.70, f32[9,256]{1,0:T(8,128)S(1)} %get-tuple-element.96, f32[1,256]{1,0:T(1,128)S(1)} %get-tuple-element.103, f32[192,256]{1,0:T(8,128)} %get-tuple-element.72, f32[192,256]{1,0:T(8,128)S(1)} %get-tuple-element.69, ...), dimensions={0} | concatenate | bytes 2420736 | tf_op jit(solution)/shard_map/concatenate | solution.py:435
  81.2 1.0 copy.44
  82.3 27.1 %sum_grads.1 = f32[2,4,4,40,256]{4,3,2,1,0:T(8,128)S(1)} custom-call(f32[2,4,4,40,256]{4,3,2,1,0:T(8,128)S(1)} %bitcast.152), custom_call_target="tpu_custom_call" | custom-call | tf_op jit(solution)/shard_map/sum_grads/pallas_call | solution.py:132
  110.1 0.9 maximum_bitcast_fusion.2
  111.6 0.9 pad_maximum_fusion
  (110 shorter events, 5.4 us)
Async XLA Ops:
  0.6 25.4 %copy-start = (bf16[768,192]{0,1:T(8,128)(2,1)S(1)}, bf16[768,192]{0,1:T(8,128)(2,1)}, u32[]{:S(2)}) copy-start(bf16[768,192]{0,1:T(8,128)(2,1)} %param.14) | copy-start | bytes 884740
  2.9 23.0 %copy-start.8 = (f32[768]{0:T(1024)}, f32[768]{0:T(1024)S(1)}, u32[]{:S(2)}) copy-start(f32[768]{0:T(1024)S(1)} %get-tuple-element.39) | copy-start | bytes 9220
  2.9 23.0 %copy-start.10 = (f32[768]{0:T(1024)}, f32[768]{0:T(1024)S(1)}, u32[]{:S(2)}) copy-start(f32[768]{0:T(1024)S(1)} %get-tuple-element.40) | copy-start | bytes 9220
  2.9 23.0 %copy-start.12 = (f32[768]{0:T(1024)}, f32[768]{0:T(1024)S(1)}, u32[]{:S(2)}) copy-start(f32[768]{0:T(1024)S(1)} %get-tuple-element.41) | copy-start | bytes 9220
  2.9 23.0 %copy-start.14 = (f32[768]{0:T(1024)}, f32[768]{0:T(1024)S(1)}, u32[]{:S(2)}) copy-start(f32[768]{0:T(1024)S(1)} %get-tuple-element.42) | copy-start | bytes 9220
  3.0 23.0 %copy-start.16 = (f32[768]{0:T(1024)}, f32[768]{0:T(1024)S(1)}, u32[]{:S(2)}) copy-start(f32[768]{0:T(1024)S(1)} %get-tuple-element.43) | copy-start | bytes 9220
  3.0 23.0 %copy-start.18 = (f32[768]{0:T(1024)}, f32[768]{0:T(1024)S(1)}, u32[]{:S(2)}) copy-start(f32[768]{0:T(1024)S(1)} %get-tuple-element.44) | copy-start | bytes 9220
  3.0 23.0 %copy-start.20 = (f32[768]{0:T(1024)}, f32[768]{0:T(1024)S(1)}, u32[]{:S(2)}) copy-start(f32[768]{0:T(1024)S(1)} %get-tuple-element.45) | copy-start | bytes 9220
  3.0 23.0 %copy-start.22 = (f32[768]{0:T(1024)}, f32[768]{0:T(1024)S(1)}, u32[]{:S(2)}) copy-start(f32[768]{0:T(1024)S(1)} %get-tuple-element.46) | copy-start | bytes 9220
  3.0 23.0 %copy-start.24 = (f32[768]{0:T(1024)}, f32[768]{0:T(1024)S(1)}, u32[]{:S(2)}) copy-start(f32[768]{0:T(1024)S(1)} %get-tuple-element.47) | copy-start | bytes 9220
  4.2 5.6 %copy-start.1 = (bf16[192,8,128]{2,0,1:T(8,128)(2,1)}, bf16[192,8,128]{2,0,1:T(8,128)(2,1)S(1)}, u32[]{:S(2)}) copy-start(bf16[192,8,128]{2,0,1:T(8,128)(2,1)S(1)} %fusion.52) | copy-start | bytes 1179652
  5.8 20.2 %copy-start.4 = (bf16[192,8,128]{0,1,2:T(8,128)(2,1)}, bf16[192,8,128]{0,1,2:T(8,128)(2,1)S(1)}, u32[]{:S(2)}) copy-start(bf16[192,8,128]{0,1,2:T(8,128)(2,1)S(1)} %copy.47) | copy-start | bytes 1179652
  26.0 9.9 %copy-start.7 = (f32[768,48]{0,1:T(8,128)S(1)}, f32[768,48]{0,1:T(8,128)}, u32[]{:S(2)}) copy-start(f32[768,48]{0,1:T(8,128)} %param.12) | copy-start | bytes 442372
  26.0 10.1 %copy-start.6 = (f32[48,768]{1,0:T(8,128)S(1)}, f32[48,768]{1,0:T(8,128)}, u32[]{:S(2)}) copy-start(f32[48,768]{1,0:T(8,128)} %param.13) | copy-start | bytes 442372
  63.3 2.4 %copy-start.3 = (f32[8,128,768]{2,0,1:T(8,128)S(1)}, f32[8,128,768]{2,0,1:T(8,128)}, u32[]{:S(2)}) copy-start(f32[8,128,768]{2,0,1:T(8,128)} %get-tuple-element.105) | copy-start | bytes 9437188
  63.3 2.4 %copy-start.9 = (f32[768]{0:T(1024)S(1)}, f32[768]{0:T(1024)}, u32[]{:S(2)}) copy-start(f32[768]{0:T(1024)} %copy-done.8) | copy-start | bytes 9220
  63.3 2.4 %copy-start.11 = (f32[768]{0:T(1024)S(1)}, f32[768]{0:T(1024)}, u32[]{:S(2)}) copy-start(f32[768]{0:T(1024)} %copy-done.10) | copy-start | bytes 9220
  63.4 2.4 %copy-start.13 = (f32[768]{0:T(1024)S(1)}, f32[768]{0:T(1024)}, u32[]{:S(2)}) copy-start(f32[768]{0:T(1024)} %copy-done.12) | copy-start | bytes 9220
  63.4 2.4 %copy-start.15 = (f32[768]{0:T(1024)S(1)}, f32[768]{0:T(1024)}, u32[]{:S(2)}) copy-start(f32[768]{0:T(1024)} %copy-done.14) | copy-start | bytes 9220
  63.4 2.4 %copy-start.17 = (f32[768]{0:T(1024)S(1)}, f32[768]{0:T(1024)}, u32[]{:S(2)}) copy-start(f32[768]{0:T(1024)} %copy-done.16) | copy-start | bytes 9220
  63.4 2.4 %copy-start.19 = (f32[768]{0:T(1024)S(1)}, f32[768]{0:T(1024)}, u32[]{:S(2)}) copy-start(f32[768]{0:T(1024)} %copy-done.18) | copy-start | bytes 9220
  63.4 2.4 %copy-start.21 = (f32[768]{0:T(1024)S(1)}, f32[768]{0:T(1024)}, u32[]{:S(2)}) copy-start(f32[768]{0:T(1024)} %copy-done.20) | copy-start | bytes 9220
  63.4 2.4 %copy-start.23 = (f32[768]{0:T(1024)S(1)}, f32[768]{0:T(1024)}, u32[]{:S(2)}) copy-start(f32[768]{0:T(1024)} %copy-done.22) | copy-start | bytes 9220
  63.4 2.4 %copy-start.25 = (f32[768]{0:T(1024)S(1)}, f32[768]{0:T(1024)}, u32[]{:S(2)}) copy-start(f32[768]{0:T(1024)} %copy-done.24) | copy-start | bytes 9220
  70.8 2.9 %copy-start.26 = (f32[192]{0:T(256)S(1)}, f32[192]{0:T(256)}, u32[]{:S(2)}) copy-start(f32[192]{0:T(256)} %param.9) | copy-start | bytes 2308
  73.6 7.3 %copy-start.2 = (bf16[1,192,8,128]{3,2,1,0:T(8,128)(2,1)S(1)}, bf16[1,192,8,128]{3,2,1,0:T(8,128)(2,1)}, u32[]{:S(2)}) copy-start(bf16[1,192,8,128]{3,2,1,0:T(8,128)(2,1)} %param.8) | copy-start | bytes 1179652
  73.6 7.3 %copy-start.5 = (bf16[1,192,8,128]{3,2,1,0:T(8,128)(2,1)S(1)}, bf16[1,192,8,128]{3,2,1,0:T(8,128)(2,1)}, u32[]{:S(2)}) copy-start(bf16[1,192,8,128]{3,2,1,0:T(8,128)(2,1)} %param.15) | copy-start | bytes 1179652

commit v5 on v3

--- a/solution.py
+++ b/solution.py
@@ -112,7 +112,7 @@
 
 
 def chunk_of(wide):
-    return 256 if wide % 256 == 0 else wide
+    return 128 if wide % 128 == 0 else wide
 
 
 def sum_all(values):

time: 108 us -> 108 us (level)
  no operation moved by 1% of the time
where the time goes in v5:
time: 108 us
  Pallas kernels  56.3 us (52%)
  other arithmetic  22.9 us (21%)
  matrix products  14.8 us (14%)
  local copies, waits for them, and re-layouts  12.4 us (11%)
  between operations  1.26 us (1%)
    pallas_call x1, Pallas kernels, sum_all(): pl.pallas_call(sum_kernel, out_shape=jax.ShapeDtypeStruct(laid.shape, f32...  31.8 us
    pallas_call x2, Pallas kernels, with_halo(): pl.pallas_call(halo_kernel, out_shape=[jax.ShapeDtypeStruct(edge_rows.sha...  19.6 us
    another operation x2, other arithmetic  6.06 us
    reduce_sum x1, other arithmetic, local(): jnp.sum(grad_conv.astype(jnp.float32) * hidden_pad[:, :, drow:drow + rows...  5.39 us
    pallas_call x1, Pallas kernels, sample_sum(): pl.pallas_call(sample_kernel, out_shape=jax.ShapeDtypeStruct(values.shape...  4.91 us
    dot_general x1, matrix products, local(): jnp.einsum('bchw,ec->behw', cotangent, w_project, preferred_element_type=...  4.9 us
    broadcast_in_dim x2, other arithmetic, with_halo(): return jnp.concatenate([left, mid, right], axis=1).transpose(2, 0, 1)[None]  4.79 us
    dot_general x1, matrix products, expand(): jnp.einsum('bchw,ce->behw', scaled, w_expand, preferred_element_type=jnp....  3.54 us

profile of v5, /device:TPU:0, one launch (start us, length us, event | category | flops | bytes accessed | tf_op | source)
XLA Modules:
  0.0 107.7 jit_solution(3934790065541233706)
XLA Ops:
  0.7 1.1 %fusion.51 = f32[8,128]{1,0:T(8,128)S(1)} fusion(bf16[1,192,8,128]{3,2,1,0:T(8,128)(2,1)} %param.8), kind=kLoop, calls=%fused_computation.82 | loop fusion | flops 588800 | bytes 397312 | tf_op jit(solution)/shard_map/reduce_sum | solution.py:297
  1.8 1.1 %slice_reduce_fusion.8 = (f32[768]{0:T(1024)S(1)}, f32[768]{0:T(1024)S(1)}, f32[768]{0:T(1024)S(1)}, f32[768]{0:T(1024)S(1)}, f32[768]{0:T(1024)S(1)}, /*index=5...) fusion(f32[768,9]{0,1:T(8,128)} %param.11), kind=kLoop, calls=%fused_computation.143 | loop fusion | bytes 55296 | tf_op jit(solution)/shard_map/slice | solution.py:313
  2.9 1.1 %fusion.52 = bf16[192,8,128]{2,0,1:T(8,128)(2,1)S(1)} fusion(f32[192]{0:T(256)} %param.9, f32[8,128]{1,0:T(8,128)S(1)} %add_rsqrt_fusion, bf16[1,192,8,128]{3,2,1,0:T(8,128)(2,1)} %param.8), kind=kLoop, calls=%fused_computation.88 | loop fusion | flops 786432 | bytes 791296 | tf_op jit(solution)/shard_map/reshape.5
  4.1 1.6 %copy.47 = bf16[192,8,128]{0,1,2:T(8,128)(2,1)S(1)} copy(bf16[192,8,128]{2,1,0:T(8,128)(2,1)} %bitcast.150) | data formatting | bytes 786432 | tf_op jit(solution)/shard_map/reshape.24
  6.1 3.5 %multiply_convert_fusion.1 = (bf16[8,128,768]{2,0,1:T(8,128)(2,1)S(1)}, f32[8,128,768]{2,0,1:T(8,128)}) fusion(bf16[192,8,128]{0,1,2:T(8,128)(2,1)S(1)} %copy.45, bf16[192,768]{1,0:T(8,128)(2,1)} %param.10), kind=kOutput, calls=%fused_computation.53 | convolution fusion | flops 305922048 | bytes 5406720 | tf_op jit(solution)/shard_map/bchw,ce->behw/dot_general | solution.py:304
  10.2 0.9 pad_maximum_fusion
  11.2 10.7 %halo.2 = (bf16[2,128,768]{2,1,0:T(8,128)(2,1)S(1)}, bf16[6,16,768]{2,1,0:T(8,128)(2,1)S(1)}) custom-call(bf16[2,128,768]{2,1,0:T(8,128)(2,1)S(1)} %copy.19.rows_ref, bf16[2,16,768]{2,1,0:T(8,128)(2,1)S(1)} %fusion.63.cols_ref), custom_call_target="tpu_custom_call" | custom-call | tf_op jit(solution)/shard_map/halo/pallas_call | solution.py:209
  22.4 0.9 broadcast_select_fusion.3
  23.3 2.5 %maximum_bitcast_fusion = bf16[1,768,10,130]{1,2,3,0:T(8,128)(2,1)S(1)} fusion(bf16[10,1,768]{2,0,1:T(8,128)(2,1)S(1)} %get-tuple-element.89, bf16[1,128,768]{2,0,1:T(2,128)(2,1)S(1)} %get-tuple-element.66, bf16[8,128,768]{2,0,1:T(8,128)(2,1)S(1)} %get-tuple-element.82, bf16[1,128,768]{2,0,1:T(2,128)(2,1)S(1)} %get-tuple-element.65, ...), kind=kLoop, calls=%fused_computation.18 | loop fusion | flops 9984000 | bytes 3993600 | tf_op jit(solution)/shard_map/broadcast_in_dim | solution.py:236
  25.8 4.9 %fusion.73 = (f32[768]{0:T(1024)S(1)}, f32[768]{0:T(1024)S(1)}, f32[1,768,8,128]{1,2,3,0:T(8,128)S(1)}, f32[768,8,128]{0,1,2:T(8,128)S(1)}) fusion(bf16[1,768,10,130]{1,2,3,0:T(8,128)(2,1)S(1)} %maximum_bitcast_fusion, f32[768]{0:T(1024)S(1)} %get-tuple-element.44, f32[768]{0:T(1024)S(1)} %get-tuple-element.45, f32[768]{0:T(1024)S(1)} %get-tuple-element.38, ...), kind=kOutput, calls=%fused_computation.153 | convolution fusion | flops 327940608 | bytes 21169152 | tf_op jit(solution)/shard_map/bchw,ec->behw/dot_general | solution.py:328
  30.8 4.9 %sample_sum.1 = f32[2,768]{1,0:T(2,128)S(1)} custom-call(f32[2,768]{1,0:T(2,128)S(1)} %pad_maximum_fusion.2.v_ref), custom_call_target="tpu_custom_call" | custom-call | tf_op jit(solution)/shard_map/sample_sum/pallas_call | solution.py:273
  36.7 5.4 %fusion.16 = (f32[768]{0:T(1024)S(1)}, f32[768]{0:T(1024)S(1)}, f32[768]{0:T(1024)S(1)}, f32[768]{0:T(1024)S(1)}, f32[768]{0:T(1024)S(1)}, /*index=5*/f32[768]{0...) fusion(bf16[1,768,10,130]{1,2,3,0:T(8,128)(2,1)S(1)} %maximum_b, ...), kind=kLoop, calls=%fused_computation.36 | loop fusion | flops 33023232 | bytes 23632896 | tf_op jit(solution)/shard_map/reduce_sum | solution.py:364
  42.2 1.3 %convolution_bitcast_fusion.2 = f32[192,768]{1,0:T(8,128)} fusion(bf16[768,8,128]{0,1,2:T(8,128)(2,1)S(1)} %get-tuple-element.50, bf16[192,8,128]{0,1,2:T(8,128)(2,1)S(1)} %copy.47), kind=kOutput, calls=%fused_computation.62 | convolution fusion | flops 301989888 | bytes 2555904 | tf_op jit(solution)/shard_map/bchw,behw->ce/dot_general | solution.py:342
  43.6 0.7 fusion.36
  44.3 1.0 copy.43
  45.3 0.7 multiply_multiply_fusion.1
  46.1 0.7 multiply_multiply_fusion
  47.3 0.9 pad_maximum_fusion.1
  48.3 8.9 %halo.3 = (bf16[2,128,768]{2,1,0:T(8,128)(2,1)S(1)}, bf16[6,16,768]{2,1,0:T(8,128)(2,1)S(1)}) custom-call(bf16[2,128,768]{2,1,0:T(8,128)(2,1)S(1)} %copy.30.rows_ref, bf16[2,16,768]{2,1,0:T(8,128)(2,1)S(1)} %fusion.64.cols_ref), custom_call_target="tpu_custom_call" | custom-call | tf_op jit(solution)/shard_map/halo/pallas_call | solution.py:209
  57.8 0.9 broadcast_select_fusion.2
  58.7 2.3 %maximum_bitcast_fusion.1 = bf16[1,768,10,130]{1,2,3,0:T(8,128)(2,1)S(1)} fusion(bf16[10,1,768]{2,0,1:T(8,128)(2,1)S(1)} %maximum_select_fusion.3, bf16[1,128,768]{2,0,1:T(2,128)(2,1)S(1)} %get-tuple-element.64, bf16[8,128,768]{2,0,1:T(8,128)(2,1)S(1)} %bitcast.149, bf16[1,128,768]{2,0,1:T(2,128)(2,1)S(1)} %get-tuple-element.63, ...), kind=kLoop, calls=%fused_computation.19 | loop fusion | flops 9984000 | bytes 3993600 | tf_op jit(solution)/shard_map/broadcast_in_dim | solution.py:236
  61.0 4.9 %fusion.29 = bf16[768,8,128]{0,1,2:T(8,128)(2,1)S(1)} fusion(f32[8,128,768]{2,0,1:T(8,128)S(1)} %copy-done.4, bf16[1,768,10,130]{1,2,3,0:T(8,128)(2,1)S(1)} %maximum_bitcast_fusion.1, f32[768]{0:T(1024)S(1)} %get-tuple-element.44, f32[768]{0:T(1024)S(1)} %get-tuple-element.45, f32[768]{0:T(1024)S(1)} %get-tuple-element.38, f32[768]{0:T(1024)S(1)} %get-tuple-element.39, ...), kind=kLoop, calls=%fused_computation.57 | loop fusion | flops 27525120 | bytes 18902016 | tf_op jit(solution)/shard_map/reshape.51
  66.0 1.2 %copy.38 = bf16[768,8,128]{2,0,1:T(8,128)(2,1)S(1)} copy(bf16[768,8,128]{0,1,2:T(8,128)(2,1)S(1)} %fusion.29) | data formatting | bytes 3145728 | tf_op jit(solution)/shard_map/reshape.51
  67.2 1.7 %convolution_bitcast_fusion.1 = f32[192,768]{1,0:T(8,128)S(1)} fusion(bf16[192,8,128]{2,0,1:T(8,128)(2,1)} %copy-done.1, bf16[768,8,128]{2,0,1:T(8,128)(2,1)S(1)} %copy.38), kind=kOutput, calls=%fused_computation.61 | convolution fusion | flops 301989888 | bytes 2555904 | tf_op jit(solution)/shard_map/bchw,behw->ce/dot_general | solution.py:372
  68.9 1.8 %fusion.50 = (f32[192]{0:T(256)S(1)}, f32[8,128]{1,0:T(8,128)S(1)}, f32[1,192,8,128]{3,1,2,0:T(8,128)S(1)}) fusion(f32[8,128]{1,0:T(8,128)S(1)} %add_rsqrt_fusion, bf16[1,192,8,128]{3,2,1,0:T(8,128)(2,1)} %param.8, f32[192]{0:T(256)S(1)} %copy-done.11, bf16[768,8,128]{2,0,1:T(8,128)(2,1)S(1)} %copy.38, bf16[192,768]{1,0:T(8,128)(2,1)} %param.10), kind=kOutput, calls=%fused_computation.81 | convolution fusion | flops 303364928 | bytes 3057152 | tf_op jit(solution)/shard_map/ce,behw->bchw/dot_general | solution.py:373
  71.0 1.0 copy.44
  72.0 0.8 concatenate.79
  72.9 31.8 %sum_grads.1 = f32[2,4,4,16,768]{4,3,2,1,0:T(8,128)S(1)} custom-call(f32[2,4,4,16,768]{4,3,2,1,0:T(8,128)S(1)} %bitcast.142), custom_call_target="tpu_custom_call" | custom-call | tf_op jit(solution)/shard_map/sum_grads/pallas_call | solution.py:129
  104.7 0.6 slice.317
  105.3 0.6 slice_bitcast_fusion.2
  105.9 0.7 fusion.77
  106.6 1.1 %slice_bitcast_fusion = (f32[768,192]{0,1:T(8,128)}, f32[192,768]{1,0:T(8,128)}) fusion(f32[512,768]{1,0:T(8,128)S(1)} %bitcast.146), kind=kLoop, calls=%fused_computation.87 | loop fusion | bytes 2359296 | tf_op jit(solution)/shard_map/transpose | solution.py:396
  (69 shorter events, 4.0 us)
Async XLA Ops:
  0.6 25.2 %copy-start = (bf16[768,192]{0,1:T(8,128)(2,1)S(1)}, bf16[768,192]{0,1:T(8,128)(2,1)}, u32[]{:S(2)}) copy-start(bf16[768,192]{0,1:T(8,128)(2,1)} %param.14) | copy-start | bytes 884740
  4.1 5.6 %copy-start.1 = (bf16[192,8,128]{2,0,1:T(8,128)(2,1)}, bf16[192,8,128]{2,0,1:T(8,128)(2,1)S(1)}, u32[]{:S(2)}) copy-start(bf16[192,8,128]{2,0,1:T(8,128)(2,1)S(1)} %fusion.52) | copy-start | bytes 1179652
  25.8 9.9 %copy-start.8 = (f32[768,48]{0,1:T(8,128)S(1)}, f32[768,48]{0,1:T(8,128)}, u32[]{:S(2)}) copy-start(f32[768,48]{0,1:T(8,128)} %param.12) | copy-start | bytes 442372
  25.8 10.1 %copy-start.7 = (f32[48,768]{1,0:T(8,128)S(1)}, f32[48,768]{1,0:T(8,128)}, u32[]{:S(2)}) copy-start(f32[48,768]{1,0:T(8,128)} %param.13) | copy-start | bytes 442372
  36.7 6.9 %copy-start.2 = (bf16[1,192,8,128]{3,2,1,0:T(8,128)(2,1)S(1)}, bf16[1,192,8,128]{3,2,1,0:T(8,128)(2,1)}, u32[]{:S(2)}) copy-start(bf16[1,192,8,128]{3,2,1,0:T(8,128)(2,1)} %param.8) | copy-start | bytes 1179652
  58.7 2.3 %copy-start.4 = (f32[8,128,768]{2,0,1:T(8,128)S(1)}, f32[8,128,768]{2,0,1:T(8,128)}, u32[]{:S(2)}) copy-start(f32[8,128,768]{2,0,1:T(8,128)} %get-tuple-element.83) | copy-start | bytes 9437188
  65.9 2.9 %copy-start.11 = (f32[192]{0:T(256)S(1)}, f32[192]{0:T(256)}, u32[]{:S(2)}) copy-start(f32[192]{0:T(256)} %param.9) | copy-start | bytes 2308
  67.1 3.6 %copy-start.3 = (bf16[1,192,8,128]{3,2,1,0:T(8,128)(2,1)S(1)}, bf16[1,192,8,128]{3,2,1,0:T(8,128)(2,1)}, u32[]{:S(2)}) copy-start(bf16[1,192,8,128]{3,2,1,0:T(8,128)(2,1)} %param.8) | copy-start | bytes 1179652
  67.1 3.6 %copy-start.6 = (bf16[1,192,8,128]{3,2,1,0:T(8,128)(2,1)S(1)}, bf16[1,192,8,128]{3,2,1,0:T(8,128)(2,1)}, u32[]{:S(2)}) copy-start(bf16[1,192,8,128]{3,2,1,0:T(8,128)(2,1)} %param.15) | copy-start | bytes 1179652
  68.9 3.1 %copy-start.5 = (f32[192,768]{1,0:T(8,128)S(1)}, f32[192,768]{1,0:T(8,128)}, u32[]{:S(2)}) copy-start(f32[192,768]{1,0:T(8,128)} %convolution_bitcast_fusion.2) | copy-start | bytes 1769476
  68.9 3.1 %copy-start.9 = (f32[48,768]{1,0:T(8,128)S(1)}, f32[48,768]{1,0:T(8,128)}, u32[]{:S(2)}) copy-start(f32[48,768]{1,0:T(8,128)} %multiply_multiply_fusion.1) | copy-start | bytes 442372
  68.9 3.1 %copy-start.10 = (f32[48,768]{1,0:T(8,128)S(1)}, f32[48,768]{1,0:T(8,128)}, u32[]{:S(2)}) copy-start(f32[48,768]{1,0:T(8,128)} %multiply_multiply_fusion) | copy-start | bytes 442372
